TPU v7x, 32 devices: a whole 2x2x4 slice. The times are simulated.
32 devices in a mesh: rows: 2 (over x), seq: 16 (over z, y, core).
Axes of the slice: x: 2, y: 2, z: 4, core: 2. Of those that a mesh axis runs over, the one named last changes fastest.
Arguments:
- states: bfloat16 [2, 2048, 512], P('rows', 'seq'), may hold values from -6 to 6
- memory: bfloat16 [2, 128, 512], P('rows', 'seq'), may hold values from -6 to 6
- target_segments: int32 [2, 2048], P('rows', 'seq'), may hold values from 0 to 2, as said below
- memory_segments: int32 [2, 128], P('rows', 'seq'), may hold values from 0 to 2, as said below
- self_query: bfloat16 [512, 512], replicated, may hold values from -0.25 to 0.25
- self_key: bfloat16 [512, 512], replicated, may hold values from -0.25 to 0.25
- self_value: bfloat16 [512, 512], replicated, may hold values from -0.25 to 0.25
- self_out: bfloat16 [512, 512], replicated, may hold values from -1 to 1
- gain_one: float32 [512], replicated, may hold values from 0.25 to 1.75
- shift_one: float32 [512], replicated, may hold values from -1.5 to 1.5
- cross_query: bfloat16 [512, 512], replicated, may hold values from -0.25 to 0.25
- cross_key: bfloat16 [512, 512], replicated, may hold values from -0.25 to 0.25
- cross_value: bfloat16 [512, 512], replicated, may hold values from -0.25 to 0.25
- cross_out: bfloat16 [512, 512], replicated, may hold values from -1 to 1
- gain_two: float32 [512], replicated, may hold values from 0.25 to 1.75
- shift_two: float32 [512], replicated, may hold values from -1.5 to 1.5
- expand_weight: bfloat16 [512, 2048], replicated, may hold values from -0.25 to 0.25
- reduce_weight: bfloat16 [2048, 512], replicated, may hold values from -0.25 to 0.25
- gain_three: float32 [512], replicated, may hold values from 0.25 to 1.75
- shift_three: float32 [512], replicated, may hold values from -1.5 to 1.5
- output_cotangent: bfloat16 [2, 2048, 512], P('rows', 'seq'), may hold values from -6 to 6
Outputs:
- layer_output: bfloat16 [2, 2048, 512], P('rows', 'seq')
- states_grad: float32 [2, 2048, 512], P('rows', 'seq')
- memory_grad: float32 [2, 128, 512], P('rows', 'seq')
- self_query_grad: float32 [512, 512], replicated
- self_key_grad: float32 [512, 512], replicated
- self_value_grad: float32 [512, 512], replicated
- self_out_grad: float32 [512, 512], replicated
- gain_one_grad: float32 [512], replicated
- shift_one_grad: float32 [512], replicated
- cross_query_grad: float32 [512, 512], replicated
- cross_key_grad: float32 [512, 512], replicated
- cross_value_grad: float32 [512, 512], replicated
- cross_out_grad: float32 [512, 512], replicated
- gain_two_grad: float32 [512], replicated
- shift_two_grad: float32 [512], replicated
- expand_weight_grad: float32 [512, 2048], replicated
- reduce_weight_grad: float32 [2048, 512], replicated
- gain_three_grad: float32 [512], replicated
- shift_three_grad: float32 [512], replicated
Inputs may be any that keep to these rules, and one draw needn't show every extreme that they name: `target_segments`: in each row the ids never fall and each of 0, 1, 2 holds at least one position; id 0 lies within the first 127 positions and id 2 within the last 127 positions. `memory_segments`: in each row the ids never fall and each of 0, 1, 2 holds at least one position; id 0 lies within the first 7 positions and id 2 within the last 7 positions.
All inputs are finite; a program needn't handle non-finite values.
Results may differ from a plain program's by a relative error of at most 0.04.
Values may be sent and summed in bfloat16 or wider, within the bound.
A program may use at most 320 MiB of HBM per device.

v0:
```python
import jax
import jax.numpy as jnp
from jax import lax
from jax.sharding import PartitionSpec as P

HEADS = 8
HEAD_DIM = 64


def layer_norm(hidden, gain, shift):
    center = hidden - jnp.mean(hidden, axis=-1, keepdims=True)
    spread = jnp.mean(center * center, axis=-1, keepdims=True)
    return center * lax.rsqrt(spread + 1e-05) * gain + shift


def split_heads(values):
    return values.reshape(values.shape[0], HEADS, HEAD_DIM)


def forward_dot(left, right):
    return jnp.dot(left, right, preferred_element_type=jnp.float32)


def outer(left, right):
    return lax.dot_general(
        left, right, (((0,), (0,)), ((), ())), preferred_element_type=jnp.float32
    )


def backward_dot(grad, weight):
    return lax.dot_general(
        grad, weight, (((1,), (1,)), ((), ())), preferred_element_type=jnp.float32
    )


def body(
    states,
    memory,
    target_segments,
    memory_segments,
    self_query,
    self_key,
    self_value,
    self_out,
    gain_one,
    shift_one,
    cross_query,
    cross_key,
    cross_value,
    cross_out,
    gain_two,
    shift_two,
    expand_weight,
    reduce_weight,
    gain_three,
    shift_three,
    output_cotangent,
):
    scale = HEAD_DIM ** (-0.5)
    low_type = jnp.bfloat16
    tokens = states[0]
    local_memory = memory[0]
    query_seg = target_segments[0]
    memory_seg = memory_segments[0]
    count = tokens.shape[0]
    own_start = lax.axis_index("seq") * count
    query_pos = own_start + jnp.arange(count, dtype=jnp.int32)
    queries = forward_dot(tokens, self_query).astype(low_type)
    keys = forward_dot(tokens, self_key).astype(low_type)
    values = forward_dot(tokens, self_value).astype(low_type)
    query_heads = split_heads(queries)
    key_heads = split_heads(keys)
    value_heads = split_heads(values)
    start_state = (
        jnp.full((count, HEADS), -1e30, jnp.float32),
        jnp.zeros((count, HEADS), jnp.float32),
        jnp.zeros((count, HEADS, HEAD_DIM), jnp.float32),
    )
    piece_keys = lax.all_gather(keys, "seq", axis=0, tiled=True)
    piece_values = lax.all_gather(values, "seq", axis=0, tiled=True)
    piece_seg = lax.all_gather(query_seg, "seq", axis=0, tiled=True)
    width = piece_keys.shape[0]
    key_pos = jnp.arange(width, dtype=jnp.int32)
    skip = (
        (jnp.int32(0) > query_pos[-1])
        | (piece_seg[-1] < query_seg[0])
        | (piece_seg[0] > query_seg[-1])
    )

    def compute(state):
        top, total, accum = state
        allowed = (
            (query_seg[:, None] == piece_seg[None, :]) & (key_pos[None, :] <= query_pos[:, None])
        )[:, None, :]
        scores = (
            jnp.einsum(
                "qhd,khd->qhk",
                query_heads,
                split_heads(piece_keys),
                preferred_element_type=jnp.float32,
            )
            * scale
        )
        scores = jnp.where(allowed, scores, -1e30)
        new_top = jnp.maximum(top, jnp.max(scores, axis=2))
        weights = jnp.where(allowed, jnp.exp(scores - new_top[:, :, None]), 0.0)
        total = jnp.sum(weights, axis=2)
        accum = jnp.einsum(
            "qhk,khd->qhd",
            weights.astype(low_type),
            split_heads(piece_values),
            preferred_element_type=jnp.float32,
        )
        return (new_top, total, accum)

    top, total, accum = lax.cond(skip, lambda state: state, compute, start_state)
    attended = accum / total[:, :, None]
    log_total = top + jnp.log(total)
    attended_low = attended.reshape(count, HEADS * HEAD_DIM).astype(low_type)
    first, back_one = jax.vjp(
        layer_norm,
        tokens.astype(jnp.float32) + forward_dot(attended_low, self_out),
        gain_one,
        shift_one,
    )
    first_low = first.astype(low_type)
    cross_q = forward_dot(first_low, cross_query).astype(low_type)
    memory_keys = forward_dot(local_memory, cross_key).astype(low_type)
    memory_values = forward_dot(local_memory, cross_value).astype(low_type)
    all_keys, all_values, all_seg = (
        lax.all_gather(memory_keys, "seq", axis=0, tiled=True),
        lax.all_gather(memory_values, "seq", axis=0, tiled=True),
        lax.all_gather(memory_seg, "seq", axis=0, tiled=True),
    )
    cross_heads = split_heads(cross_q)
    mem_key_heads = split_heads(all_keys)
    mem_value_heads = split_heads(all_values)
    cross_allowed = (query_seg[:, None] == all_seg[None, :])[:, None, :]
    cross_scores = (
        jnp.einsum("qhd,khd->qhk", cross_heads, mem_key_heads, preferred_element_type=jnp.float32)
        * scale
    )
    cross_scores = jnp.where(cross_allowed, cross_scores, -1e30)
    cross_top = jnp.max(cross_scores, axis=2, keepdims=True)
    cross_weights = jnp.where(cross_allowed, jnp.exp(cross_scores - cross_top), 0.0)
    cross_total = jnp.sum(cross_weights, axis=2, keepdims=True)
    cross_probs = cross_weights / cross_total
    cross_probs_low = cross_probs.astype(low_type)
    crossed = jnp.einsum(
        "qhk,khd->qhd", cross_probs_low, mem_value_heads, preferred_element_type=jnp.float32
    )
    crossed_low = crossed.reshape(count, HEADS * HEAD_DIM).astype(low_type)
    second, back_two = jax.vjp(
        layer_norm, first + forward_dot(crossed_low, cross_out), gain_two, shift_two
    )
    second_low = second.astype(low_type)
    gate = forward_dot(second_low, expand_weight)
    hidden, silu_back = jax.vjp(jax.nn.silu, gate)
    hidden_low = hidden.astype(low_type)
    result, back_three = jax.vjp(
        layer_norm, second + forward_dot(hidden_low, reduce_weight), gain_three, shift_three
    )
    layer_output = result.astype(low_type)[None]
    d_third, gain_three_grad, shift_three_grad = back_three(output_cotangent[0].astype(jnp.float32))
    d_branch = d_third.astype(low_type)
    reduce_weight_grad = outer(hidden_low, d_branch)
    d_gate = silu_back(backward_dot(d_branch, reduce_weight))[0].astype(low_type)
    expand_weight_grad = outer(second_low, d_gate)
    d_second = d_third + backward_dot(d_gate, expand_weight)
    d_mid, gain_two_grad, shift_two_grad = back_two(d_second)
    d_cross_branch = d_mid.astype(low_type)
    cross_out_grad = outer(crossed_low, d_cross_branch)
    d_crossed = split_heads(backward_dot(d_cross_branch, cross_out).astype(low_type))
    d_probs = jnp.einsum(
        "qhd,khd->qhk", d_crossed, mem_value_heads, preferred_element_type=jnp.float32
    )
    cross_delta = jnp.sum(cross_probs * d_probs, axis=2, keepdims=True)
    d_scores = (cross_probs * (d_probs - cross_delta)).astype(low_type)
    d_cross_q = (
        (
            jnp.einsum("qhk,khd->qhd", d_scores, mem_key_heads, preferred_element_type=jnp.float32)
            * scale
        )
        .reshape(count, HEADS * HEAD_DIM)
        .astype(low_type)
    )
    key_terms = (
        jnp.einsum("qhk,qhd->khd", d_scores, cross_heads, preferred_element_type=jnp.float32)
        * scale
    ).reshape(-1, HEADS * HEAD_DIM)
    value_terms = jnp.einsum(
        "qhk,qhd->khd", cross_probs_low, d_crossed, preferred_element_type=jnp.float32
    ).reshape(-1, HEADS * HEAD_DIM)
    d_mem_keys, d_mem_values = (
        lax.psum_scatter(key_terms, "seq", scatter_dimension=0, tiled=True),
        lax.psum_scatter(value_terms, "seq", scatter_dimension=0, tiled=True),
    )
    d_mem_keys = d_mem_keys.astype(low_type)
    d_mem_values = d_mem_values.astype(low_type)
    cross_key_grad = outer(local_memory, d_mem_keys)
    cross_value_grad = outer(local_memory, d_mem_values)
    memory_grad = (backward_dot(d_mem_keys, cross_key) + backward_dot(d_mem_values, cross_value))[
        None
    ]
    cross_query_grad = outer(first_low, d_cross_q)
    d_first = d_mid + backward_dot(d_cross_q, cross_query)
    d_start, gain_one_grad, shift_one_grad = back_one(d_first)
    d_self_branch = d_start.astype(low_type)
    self_out_grad = outer(attended_low, d_self_branch)
    d_attended = backward_dot(d_self_branch, self_out).astype(low_type)
    d_heads = split_heads(d_attended)
    delta = jnp.sum(d_heads.astype(jnp.float32) * attended, axis=2)
    all_log, all_delta = (
        lax.all_gather(log_total, "seq", axis=0, tiled=True),
        lax.all_gather(delta, "seq", axis=0, tiled=True),
    )

    def query_part(total_q, piece_keys, piece_values, piece_seg, start):
        key_pos = start + jnp.arange(piece_keys.shape[0], dtype=jnp.int32)
        allowed = (
            (query_seg[:, None] == piece_seg[None, :]) & (key_pos[None, :] <= query_pos[:, None])
        )[:, None, :]
        piece_key_heads = split_heads(piece_keys)
        scores = (
            jnp.einsum(
                "qhd,khd->qhk", query_heads, piece_key_heads, preferred_element_type=jnp.float32
            )
            * scale
        )
        scores = jnp.where(allowed, scores, -1e30)
        probs = jnp.where(allowed, jnp.exp(scores - log_total[:, :, None]), 0.0)
        grads_p = jnp.einsum(
            "qhd,khd->qhk", d_heads, split_heads(piece_values), preferred_element_type=jnp.float32
        )
        grads_s = (probs * (grads_p - delta[:, :, None])).astype(low_type)
        return (
            total_q
            + jnp.einsum(
                "qhk,khd->qhd", grads_s, piece_key_heads, preferred_element_type=jnp.float32
            )
            * scale
        )

    def key_part(
        grad_k, grad_v, piece_queries, piece_grads, piece_seg, piece_log, piece_delta, start
    ):
        piece_pos = start + jnp.arange(piece_queries.shape[0], dtype=jnp.int32)
        allowed = (
            (piece_seg[:, None] == query_seg[None, :]) & (query_pos[None, :] <= piece_pos[:, None])
        )[:, None, :]
        piece_query_heads = split_heads(piece_queries)
        piece_grad_heads = split_heads(piece_grads)
        scores = (
            jnp.einsum(
                "qhd,khd->qhk", piece_query_heads, key_heads, preferred_element_type=jnp.float32
            )
            * scale
        )
        scores = jnp.where(allowed, scores, -1e30)
        probs = jnp.where(allowed, jnp.exp(scores - piece_log[:, :, None]), 0.0)
        grad_v = grad_v + jnp.einsum(
            "qhk,qhd->khd",
            probs.astype(low_type),
            piece_grad_heads,
            preferred_element_type=jnp.float32,
        )
        grads_p = jnp.einsum(
            "qhd,khd->qhk", piece_grad_heads, value_heads, preferred_element_type=jnp.float32
        )
        grads_s = (probs * (grads_p - piece_delta[:, :, None])).astype(low_type)
        grad_k = (
            grad_k
            + jnp.einsum(
                "qhk,qhd->khd", grads_s, piece_query_heads, preferred_element_type=jnp.float32
            )
            * scale
        )
        return (grad_k, grad_v)

    zeros_heads = jnp.zeros((count, HEADS, HEAD_DIM), jnp.float32)
    own_q = query_part(zeros_heads, keys, values, query_seg, own_start)
    own_k, own_v = key_part(
        zeros_heads, zeros_heads, queries, d_attended, query_seg, log_total, delta, own_start
    )

    def both_sides(grads, piece):
        piece_keys, piece_values, piece_queries, piece_grads, piece_seg = piece
        shards = piece_keys.shape[0] // count

        def one_shard(number, state):
            shard_start = number * count

            def rows_of(array):
                return lax.dynamic_slice_in_dim(array, number * count, count, 0)

            shard_seg = rows_of(piece_seg)
            far = (
                (shard_seg[-1] < query_seg[0])
                | (shard_seg[0] > query_seg[-1])
                | (shard_start == own_start)
            )
            branch = jnp.where(far, 0, jnp.where(shard_start < own_start, 1, 2)).astype(jnp.int32)

            def keep_state(inner):
                return inner

            def query_branch(inner):
                return (
                    query_part(
                        inner[0], rows_of(piece_keys), rows_of(piece_values), shard_seg, shard_start
                    ),
                    inner[1],
                    inner[2],
                )

            def key_branch(inner):
                shard_log = lax.dynamic_slice_in_dim(all_log, shard_start, count, 0)
                shard_delta = lax.dynamic_slice_in_dim(all_delta, shard_start, count, 0)
                new_k, new_v = key_part(
                    inner[1],
                    inner[2],
                    rows_of(piece_queries),
                    rows_of(piece_grads),
                    shard_seg,
                    shard_log,
                    shard_delta,
                    shard_start,
                )
                return (inner[0], new_k, new_v)

            return lax.switch(branch, [keep_state, query_branch, key_branch], state)

        return lax.fori_loop(0, shards, one_shard, grads)

    grad_q, grad_k, grad_v = both_sides(
        (own_q, own_k, own_v),
        (
            lax.all_gather(keys, "seq", axis=0, tiled=True),
            lax.all_gather(values, "seq", axis=0, tiled=True),
            lax.all_gather(queries, "seq", axis=0, tiled=True),
            lax.all_gather(d_attended, "seq", axis=0, tiled=True),
            lax.all_gather(query_seg, "seq", axis=0, tiled=True),
        ),
    )
    grad_q = grad_q.reshape(count, HEADS * HEAD_DIM).astype(low_type)
    grad_k = grad_k.reshape(count, HEADS * HEAD_DIM).astype(low_type)
    grad_v = grad_v.reshape(count, HEADS * HEAD_DIM).astype(low_type)
    self_query_grad = outer(tokens, grad_q)
    self_key_grad = outer(tokens, grad_k)
    self_value_grad = outer(tokens, grad_v)
    states_grad = (
        d_start
        + backward_dot(grad_q, self_query)
        + backward_dot(grad_k, self_key)
        + backward_dot(grad_v, self_value)
    )[None]
    summed = lax.psum(
        (
            self_query_grad,
            self_key_grad,
            self_value_grad,
            self_out_grad,
            gain_one_grad,
            shift_one_grad,
            cross_query_grad,
            cross_key_grad,
            cross_value_grad,
            cross_out_grad,
            gain_two_grad,
            shift_two_grad,
            expand_weight_grad,
            reduce_weight_grad,
            gain_three_grad,
            shift_three_grad,
        ),
        ("rows", "seq"),
    )
    (
        self_query_grad,
        self_key_grad,
        self_value_grad,
        self_out_grad,
        gain_one_grad,
        shift_one_grad,
    ) = summed[0:6]
    (
        cross_query_grad,
        cross_key_grad,
        cross_value_grad,
        cross_out_grad,
        gain_two_grad,
        shift_two_grad,
    ) = summed[6:12]
    expand_weight_grad, reduce_weight_grad, gain_three_grad, shift_three_grad = summed[12:16]
    return (
        layer_output,
        states_grad,
        memory_grad,
        self_query_grad,
        self_key_grad,
        self_value_grad,
        self_out_grad,
        gain_one_grad,
        shift_one_grad,
        cross_query_grad,
        cross_key_grad,
        cross_value_grad,
        cross_out_grad,
        gain_two_grad,
        shift_two_grad,
        expand_weight_grad,
        reduce_weight_grad,
        gain_three_grad,
        shift_three_grad,
    )


def solution(mesh):
    return jax.shard_map(
        body,
        mesh=mesh,
        in_specs=(
            P("rows", "seq", None),
            P("rows", "seq", None),
            P("rows", "seq"),
            P("rows", "seq"),
            P(),
            P(),
            P(),
            P(),
            P(),
            P(),
            P(),
            P(),
            P(),
            P(),
            P(),
            P(),
            P(),
            P(),
            P(),
            P(),
            P("rows", "seq", None),
        ),
        out_specs=(
            P("rows", "seq", None),
            P("rows", "seq", None),
            P("rows", "seq", None),
            P(),
            P(),
            P(),
            P(),
            P(),
            P(),
            P(),
            P(),
            P(),
            P(),
            P(),
            P(),
            P(),
            P(),
            P(),
            P(),
        ),
        check_vma=False,
    )
```

profile of v0, /device:TPU:0, one launch (start us, length us, event | category | flops | bytes accessed | tf_op | source)
XLA Modules:
  0.0 859.0 jit_solution(14068849716861711452)
XLA Ops:
  13.6 23.8 %all-gather = s32[1,2048]{1,0:T(1,128)} all-gather(s32[1,128]{1,0:T(1,128)} %param.30), channel_id=2, replica_groups=mesh['rows'=2,'seq'=16] {'seq'}, dimensions={1}, use_global_device_ids=true | all-gather | bytes 8704 | tf_op jit(solution)/shard_map/all_gather | solution.py:81
  41.0 17.9 %all_gather.36 = bf16[128,512]{1,0:T(8,128)(2,1)S(1)} all-gather(bf16[8,512]{1,0:T(8,128)(2,1)S(1)} %convolution_convert_fusion.8), channel_id=1, replica_groups=mesh['rows'=2,'seq'=16] {'seq'}, dimensions={0}, use_global_device_ids=true | all-gather | bytes 139264 | tf_op jit(solution)/shard_map/all_gather | solution.py:132
  60.9 19.1 %all_gather.38 = bf16[128,512]{1,0:T(8,128)(2,1)S(1)} all-gather(bf16[8,512]{1,0:T(8,128)(2,1)S(1)} %convolution_convert_fusion.7), channel_id=1, replica_groups=mesh['rows'=2,'seq'=16] {'seq'}, dimensions={0}, use_global_device_ids=true | all-gather | bytes 139264 | tf_op jit(solution)/shard_map/all_gather | solution.py:131
  87.2 8.2 all-reduce
  97.7 24.1 %conditional.2 = (f32[128,8]{0,1:T(8,128)S(1)}, f32[128,8]{0,1:T(8,128)S(1)}, f32[128,8,64]{0,2,1:T(8,128)S(1)}, f32[128,8]{0,1:T(8,128)}) conditional(s32[]{:T(128)} %convert_element_type.140, (s32[1,128]{1,0:T(1,128)S(1)}, s32[2048]{0:T(1024)}, s32[2048]{0:T(1024)S(1)}, s32[128]{0:T(128)S(1)}, bf16[2048,512]{1,0:T(8,128)(2,1)}, ...), branch_computations={%region_0.3_spmd, %region_3.4_spmd} | conditional | flops 564919296 | bytes 72795200 | solution.py:116
  163.7 21.8 %all_gather.40 = f32[2048,8]{0,1:T(8,128)} all-gather(f32[128,8]{0,1:T(8,128)} %add.223), channel_id=1, replica_groups=mesh['rows'=2,'seq'=16] {'seq'}, dimensions={0}, use_global_device_ids=true | all-gather | bytes 69632 | tf_op jit(solution)/shard_map/all_gather | solution.py:214
  185.5 19.2 %all_gather.42 = f32[2048,8]{0,1:T(8,128)} all-gather(f32[128,8]{0,1:T(8,128)S(1)} %multiply_reduce_fusion.3), channel_id=1, replica_groups=mesh['rows'=2,'seq'=16] {'seq'}, dimensions={0}, use_global_device_ids=true | all-gather | bytes 69632 | tf_op jit(solution)/shard_map/all_gather | solution.py:215
  220.0 43.4 %reduce-scatter.9.cloned.1.call-done = f32[8,512]{1,0:T(8,128)} async-done(((f32[128,512]{1,0:T(8,128)}), f32[8,512]{1,0:T(8,128)}) %reduce-scatter.9.cloned.1.call-update) | async-done | bytes 16400
  266.8 39.1 %all-gather.13.cloned.1.call-done = bf16[2048,512]{1,0:T(8,128)(2,1)} async-done(((bf16[128,512]{1,0:T(8,128)(2,1)}), bf16[2048,512]{1,0:T(8,128)(2,1)}) %all-gather.13.cloned.1.call-update) | async-done | bytes 2097168 | tf_op jit(solution)/shard_map/all_gather | solution.py:341
  309.9 179.7 %while.19 = (s32[]{:T(128)}, f32[128,8,64]{2,1,0:T(8,128)S(1)}, f32[128,8,64]{0,2,1:T(8,128)}, f32[128,8,64]{0,2,1:T(8,128)}, s32[2048]{0:T(1024)}, /*index=5*/s...) while((s32[]{:T(128)}, f32[128,8,64]{2,1,0:T(8,128)S(1)}, ...), condition=%wide.region_24.25_spmd.clone.clone, body=%wide.region_20.24_spmd.clone.clone.sunk | while | flops 68403480 | bytes 12235485 | solution.py:333
  317.8 7.8 conditional.6
  329.5 7.8 conditional.6
  352.9 7.8 conditional.6
  364.6 7.8 conditional.6
  376.3 7.8 conditional.6
  388.0 7.8 conditional.6
  411.4 7.8 conditional.6
  423.2 7.8 conditional.6
  434.9 7.8 conditional.6
  446.6 7.8 conditional.6
  470.0 7.8 conditional.6
  481.7 7.8 conditional.6
  496.7 82.9 %all-reduce.1 = (f32[512]{0:T(512)}, f32[512]{0:T(512)}, f32[512]{0:T(512)}, f32[512]{0:T(512)}, f32[512]{0:T(512)}, /*index=5*/f32[512]{0:T(512)}) all-reduce(f32[512]{0:T(512)S(1)} %copy-done.59, f32[512]{0:T(512)S(1)} %copy-done.60, f32[512]{0:T(512)} %get-tuple-element.771, ...), channel_id=1, replica_groups=mesh['rows'=2,'seq'=16] {'rows','seq'}, use_global_device_ids=true, to_apply=%region_32.33 | all-reduce | flops 3072 | bytes 24576 | tf_op jit(solution)/shard_map/psum | solution.py:357
  583.0 248.6 %all-reduce.5.cloned.1.call-done = (f32[512,512]{0,1:T(8,128)}, f32[512,512]{0,1:T(8,128)}, f32[512,512]{0,1:T(8,128)}, f32[512,512]{1,0:T(8,128)}, f32[512,512]...) async-done(((f32[512,512]{0,1:T(8,128)}, f32[512,512]{0,1:T(8,128)}, ...) | async-done | bytes 16777232 | tf_op jit(solution)/shard_map/psum | solution.py:357
  (463 shorter events, 297.4 us)
Async XLA Ops:
  7.2 127.9 %copy-start = (bf16[512,2048]{1,0:T(8,128)(2,1)S(1)}, bf16[512,2048]{1,0:T(8,128)(2,1)}, u32[]{:S(2)}) copy-start(bf16[512,2048]{1,0:T(8,128)(2,1)} %param.44) | copy-start | bytes 6291460
  7.2 78.6 %copy-start.73 = (u32[32]{0:T(128)S(1)}, u32[32]{0:T(128)}, u32[]{:S(2)}) copy-start(u32[32]{0:T(128)} %constant.123) | copy-start | bytes 388
  7.2 88.2 %copy-start.45 = (s32[1,128]{1,0:T(1,128)S(1)}, s32[1,128]{1,0:T(1,128)}, u32[]{:S(2)}) copy-start(s32[1,128]{1,0:T(1,128)} %param.30) | copy-start | bytes 1540
  7.2 79.9 %copy-start.72 = (s32[1,8]{1,0:T(1,128)S(1)}, s32[1,8]{1,0:T(1,128)}, u32[]{:S(2)}) copy-start(s32[1,8]{1,0:T(1,128)} %param.31) | copy-start | bytes 100
  7.2 88.9 %all-gather.7.cloned.1.call-start = ((), (), s32[]{:S(2)}) async-start(), calls=%async_computation.2 | async-start | bytes 2228224 | tf_op jit(solution)/shard_map/all_gather | solution.py:79
  9.4 88.3 %all-gather.9.cloned.1.call-start = ((), (), s32[]{:S(2)}) async-start(), calls=%async_computation.3 | async-start | bytes 2228224 | tf_op jit(solution)/shard_map/all_gather | solution.py:80
  11.5 148.1 %all-gather.11.cloned.1.call-start = ((), (), s32[]{:S(2)}) async-start(), calls=%async_computation.4 | async-start | bytes 2228224 | tf_op jit(solution)/shard_map/all_gather | solution.py:340
  13.6 205.4 %reduce-scatter.7.cloned.1.call-start = ((), (), s32[]{:S(2)}) async-start(), calls=%async_computation.6 | async-start | bytes 278528
  150.1 113.4 %reduce-scatter.9.cloned.1.call-start = ((), (), s32[]{:S(2)}) async-start(), calls=%async_computation.7 | async-start | bytes 278528
  150.4 56.3 %copy-start.9 = (f32[128,512]{1,0:T(8,128)}, f32[128,512]{1,0:T(8,128)S(1)}, u32[]{:S(2)}) copy-start(f32[128,512]{1,0:T(8,128)S(1)} %get-tuple-element.836) | copy-start | bytes 786436
  150.7 155.2 %all-gather.13.cloned.1.call-start = ((), (), s32[]{:S(2)}) async-start(), calls=%async_computation.5 | async-start | bytes 2228224 | tf_op jit(solution)/shard_map/all_gather | solution.py:341
  151.7 679.9 %all-reduce.5.cloned.1.call-start = ((), (), s32[]{:S(2)}) async-start(), calls=%async_computation.8 | async-start | bytes 33554432 | tf_op jit(solution)/shard_map/psum | solution.py:357
  159.6 53.0 %copy-start.22 = (bf16[128,2048]{1,0:T(8,128)(2,1)S(1)}, bf16[128,2048]{1,0:T(8,128)(2,1)}, u32[]{:S(2)}) copy-start(bf16[128,2048]{1,0:T(8,128)(2,1)} %copy-done.21) | copy-start | bytes 1572868
  159.6 53.0 %copy-start.51 = (f32[512]{0:T(512)S(1)}, f32[512]{0:T(512)}, u32[]{:S(2)}) copy-start(f32[512]{0:T(512)} %param.42) | copy-start | bytes 6148
  219.0 90.9 %copy-start.2 = (bf16[2048,512]{1,0:T(8,128)(2,1)S(1)}, bf16[2048,512]{1,0:T(8,128)(2,1)}, u32[]{:S(2)}) copy-start(bf16[2048,512]{1,0:T(8,128)(2,1)} %all-gather.7.cloned.1.call-done) | copy-start | bytes 6291460
  220.0 89.9 %copy-start.24 = (bf16[8,512]{0,1:T(8,128)(2,1)}, bf16[8,512]{0,1:T(8,128)(2,1)S(1)}, u32[]{:S(2)}) copy-start(bf16[8,512]{0,1:T(8,128)(2,1)S(1)} %copy.162) | copy-start | bytes 24580
  495.5 84.1 %copy-start.16 = (bf16[512,512]{1,0:T(8,128)(2,1)S(1)}, bf16[512,512]{1,0:T(8,128)(2,1)}, u32[]{:S(2)}) copy-start(bf16[512,512]{1,0:T(8,128)(2,1)} %param.39) | copy-start | bytes 1572868
  495.5 84.1 %copy-start.25 = (bf16[8,512]{0,1:T(8,128)(2,1)S(1)}, bf16[8,512]{0,1:T(8,128)(2,1)}, u32[]{:S(2)}) copy-start(bf16[8,512]{0,1:T(8,128)(2,1)} %copy-done.24) | copy-start | bytes 24580
  495.5 84.3 %copy-start.17 = (bf16[512,512]{1,0:T(8,128)(2,1)S(1)}, bf16[512,512]{1,0:T(8,128)(2,1)}, u32[]{:S(2)}) copy-start(bf16[512,512]{1,0:T(8,128)(2,1)} %param.40) | copy-start | bytes 1572868
  495.5 84.3 %copy-start.27 = (bf16[8,512]{0,1:T(8,128)(2,1)S(1)}, bf16[8,512]{0,1:T(8,128)(2,1)}, u32[]{:S(2)}) copy-start(bf16[8,512]{0,1:T(8,128)(2,1)} %copy-done.26) | copy-start | bytes 24580
  495.5 85.2 %copy-start.10 = (f32[128,512]{1,0:T(8,128)S(1)}, f32[128,512]{1,0:T(8,128)}, u32[]{:S(2)}) copy-start(f32[128,512]{1,0:T(8,128)} %copy-done.9) | copy-start | bytes 786436
  495.5 85.2 %copy-start.18 = (bf16[512,512]{1,0:T(8,128)(2,1)S(1)}, bf16[512,512]{1,0:T(8,128)(2,1)}, u32[]{:S(2)}) copy-start(bf16[512,512]{1,0:T(8,128)(2,1)} %param.32) | copy-start | bytes 1572868
  495.6 86.1 %copy-start.19 = (bf16[512,512]{1,0:T(8,128)(2,1)S(1)}, bf16[512,512]{1,0:T(8,128)(2,1)}, u32[]{:S(2)}) copy-start(bf16[512,512]{1,0:T(8,128)(2,1)} %param.33) | copy-start | bytes 1572868
  495.6 86.4 %copy-start.20 = (bf16[512,512]{1,0:T(8,128)(2,1)S(1)}, bf16[512,512]{1,0:T(8,128)(2,1)}, u32[]{:S(2)}) copy-start(bf16[512,512]{1,0:T(8,128)(2,1)} %param.34) | copy-start | bytes 1572868
  (71 other events, 502.0 us)
Sparse Core Ops, SparseCore 0:
  10.8 44.4 all-gather.6
  57.5 40.1 all-gather.8
  99.9 40.3 all-gather.10
  150.2 54.8 reduce-scatter.6
  209.1 54.3 reduce-scatter.8
  265.5 40.4 all-gather.12
  495.7 335.8 all-reduce.4
where the time goes:
time: 864 us; the launch traced here: 859 us
  waiting for transfers between devices  333 us (39%)
  blocking collectives  193 us (22%)
  matrix products  145 us (17%)
  local copies, waits for them, and re-layouts  102 us (12%)
  loops' own time  42.1 us (5%)
  other arithmetic  24.6 us (3%)
  between operations  19 us (2%)
    psum x1, waiting for transfers between devices, body(): lax.psum((self_query_grad, self_key_grad, self_value_grad, self_out_grad,...  249 us
    psum x1, blocking collectives, body(): lax.psum((self_query_grad, self_key_grad, self_value_grad, self_out_grad,...  82.9 us
    unnamed x9, waiting for transfers between devices  43.8 us
    another operation x1, loops' own time, both_sides(): return lax.fori_loop(0, shards, one_shard, grads)  40.8 us
    all_gather x1, waiting for transfers between devices, body(): lax.all_gather(d_attended, 'seq', axis=0, tiled=True)  39.1 us
    unnamed x166, local copies, waits for them, and re-layouts  36.2 us
    dot_general x16, matrix products, key_part(): jnp.einsum('qhk,qhd->khd', grads_s, piece_query_heads, preferred_element_...  33.6 us
    dot_general x16, matrix products, key_part(): jnp.einsum('qhk,qhd->khd', probs.astype(low_type), piece_grad_heads, pref...  28.9 us
  transfers between devices with their start and end apart: 7, of which 4 were waited for; matrix products, arithmetic and copies ran while one was open for 12% of the time, Pallas kernels for 0%

commit v1 on v0

--- a/solution.py
+++ b/solution.py
@@ -1,10 +1,294 @@
+import functools
+
 import jax
 import jax.numpy as jnp
 from jax import lax
+from jax.experimental import pallas as pl
+from jax.experimental.pallas import tpu as pltpu
 from jax.sharding import PartitionSpec as P
 
 HEADS = 8
 HEAD_DIM = 64
+MESH = pl.DeviceIdType.MESH
+LOW = jnp.bfloat16
+EXTENT = {"x": 2, "y": 2, "z": 4}
+ORDERS = (("x", "y", "z"), ("y", "x", "z"))
+
+
+def rows_at(start, size):
+    return pl.ds(pl.multiple_of(start, 16), size)
+
+
+class Place:
+    def __init__(self):
+        self.row = lax.axis_index("rows")
+        self.seq = lax.axis_index("seq")
+        self.core = lax.rem(self.seq, 2)
+        self.at = {
+            "x": self.row,
+            "y": lax.rem(self.seq // 2, 2),
+            "z": self.seq // 4,
+        }
+
+    def sibling(self):
+        return (self.row, self.seq + 1 - 2 * self.core)
+
+    def moved(self, dim, step):
+        there = lax.rem(self.at[dim] + step, EXTENT[dim])
+        if dim == "x":
+            return there, (there, self.seq)
+        weight = 2 if dim == "y" else 4
+        return there, (self.row, self.seq + (there - self.at[dim]) * weight)
+
+    def partners(self):
+        found = [self.sibling()]
+        for dim, extent in EXTENT.items():
+            found += [self.moved(dim, step)[1] for step in range(1, extent)]
+        return found
+
+
+def meet(devices):
+    barrier = pltpu.get_barrier_semaphore()
+    for device in devices:
+        pl.semaphore_signal(barrier, inc=1, device_id=device, device_id_type=MESH)
+    pl.semaphore_wait(barrier, len(devices))
+
+
+class Summed:
+    COPIES = 2 * 2 * (1 + 1 + 3) + 1
+
+    def __init__(self, place, part, landing, done, send, recv, start, size, landing_at, first):
+        self.place, self.part, self.landing, self.done = place, part, landing, done
+        self.send, self.recv = send, recv
+        self.start, self.size = start, size
+        self.sem = first
+        self.plan = []
+        half = size // 2
+        for color, order in enumerate(ORDERS):
+            steps, span = [], half
+            base = start + color * half
+            for dim in order:
+                extent = EXTENT[dim]
+                share = span // extent
+                own = base + place.at[dim] * share
+                steps.append((dim, base, span, share, own, landing_at, self.sem))
+                landing_at += share * (extent - 1)
+                self.sem += 2 * (extent - 1)
+                base, span = own, share
+            self.plan.append(steps)
+        self.last_sem = self.sem
+        self.landing_end = landing_at
+
+    def _out(self, color, step):
+        dim, base, span, share, own, at, sem = self.plan[color][step]
+        copies = []
+        for hop in range(1, EXTENT[dim]):
+            there, device = self.place.moved(dim, hop)
+            copies.append(
+                pltpu.make_async_remote_copy(
+                    src_ref=self.part.at[rows_at(base + there * share, share)],
+                    dst_ref=self.landing.at[pl.ds(at + (hop - 1) * share, share)],
+                    send_sem=self.send.at[sem + hop - 1],
+                    recv_sem=self.recv.at[sem + hop - 1],
+                    device_id=device,
+                    device_id_type=MESH,
+                )
+            )
+        return copies
+
+    def _back(self, color, step):
+        dim, base, span, share, own, at, sem = self.plan[color][step]
+        extent = EXTENT[dim]
+        copies = []
+        for hop in range(1, extent):
+            there, device = self.place.moved(dim, hop)
+            mine = self.done.at[self.place.core, rows_at(own, share)]
+            copies.append(
+                pltpu.make_async_remote_copy(
+                    src_ref=mine,
+                    dst_ref=mine,
+                    send_sem=self.send.at[sem + extent - 1 + hop - 1],
+                    recv_sem=self.recv.at[sem + extent - 1 + hop - 1],
+                    device_id=device,
+                    device_id_type=MESH,
+                )
+            )
+        return copies
+
+    def _across(self):
+        mine = self.done.at[self.place.core, pl.ds(self.start, self.size)]
+        return pltpu.make_async_remote_copy(
+            src_ref=mine,
+            dst_ref=mine,
+            send_sem=self.send.at[self.last_sem],
+            recv_sem=self.recv.at[self.last_sem],
+            device_id=self.place.sibling(),
+            device_id_type=MESH,
+        )
+
+    def begin(self):
+        for color in range(2):
+            for copy in self._out(color, 0):
+                copy.start()
+
+    def gather(self, step):
+        for color in range(2):
+            dim, base, span, share, own, at, sem = self.plan[color][step]
+            for copy in self._out(color, step):
+                copy.wait()
+            block = min(share, 128)
+
+            def add(number, carry, color=color, step=step, share=share, own=own, at=at, dim=dim, block=block):
+                rows = rows_at(own + number * block, block)
+                total = self.part[rows].astype(jnp.float32)
+                for hop in range(1, EXTENT[dim]):
+                    here = rows_at(at + (hop - 1) * share + number * block, block)
+                    total = total + self.landing[here].astype(jnp.float32)
+                if step == 2:
+                    self.done[self.place.core, rows] = total.astype(LOW)
+                else:
+                    self.part[rows] = total.astype(LOW)
+                return carry
+
+            lax.fori_loop(0, share // block, add, 0)
+            for copy in self._out(color, step + 1) if step < 2 else self._back(color, 2):
+                copy.start()
+
+    def spread(self, step):
+        for color in range(2):
+            for copy in self._back(color, step):
+                copy.wait()
+            if step > 0:
+                for copy in self._back(color, step - 1):
+                    copy.start()
+        if step == 0:
+            self._across().start()
+
+    def end(self):
+        self._across().wait()
+
+
+PIECES = (2048, 2048, 2048, 2048)
+
+
+def sum_kernel(given, small, done_out, small_out, part, landing, done, other, small_in, send, recv):
+    place = Place()
+    meet(place.partners())
+    core = place.core
+    copy = pltpu.make_async_remote_copy(
+        src_ref=given.at[1 - core],
+        dst_ref=other,
+        send_sem=send.at[0],
+        recv_sem=recv.at[0],
+        device_id=place.sibling(),
+        device_id_type=MESH,
+    )
+    copy.start()
+    small_out[...] = small[...]
+    peers = [("c", 1), ("x", 1), ("y", 1), ("z", 3)]
+    slot = 0
+    for dim, extent in peers:
+        moves = []
+        for hop in range(1, extent + 1):
+            device = place.sibling() if dim == "c" else place.moved(dim, hop)[1]
+            moves.append(
+                pltpu.make_async_remote_copy(
+                    src_ref=small_out,
+                    dst_ref=small_in.at[3 + place.at["z"] if dim == "z" else slot],
+                    send_sem=send.at[1 + slot],
+                    recv_sem=recv.at[1 + slot],
+                    device_id=device,
+                    device_id_type=MESH,
+                )
+            )
+            slot += 1
+        for move in moves:
+            move.start()
+        for move in moves:
+            move.wait()
+        if dim == "z":
+            small_in[3 + place.at["z"]] = small_out[...]
+            small_out[...] = (small_in[3] + small_in[4]) + (small_in[5] + small_in[6])
+        else:
+            small_out[...] = small_out[...] + small_in[slot - 1]
+    copy.wait()
+    pieces, start, landing_at, first = [], 0, 0, 7
+    for size in PIECES:
+        piece = Summed(place, part, landing, done, send, recv, start, size, landing_at, first)
+
+        def join(number, carry):
+            rows = rows_at(start + number * 128, 128)
+            part[rows] = (given[core, rows].astype(jnp.float32) + other[rows].astype(jnp.float32)).astype(LOW)
+            return carry
+
+        lax.fori_loop(0, size // 128, join, 0)
+        piece.begin()
+        pieces.append(piece)
+        start, landing_at, first = start + size, piece.landing_end, piece.last_sem + 1
+    for step in range(3):
+        for piece in pieces:
+            piece.gather(step)
+    for step in (2, 1, 0):
+        for piece in pieces:
+            piece.spread(step)
+    for piece in pieces:
+        piece.end()
+    done_out[...] = done[...]
+
+
+def sum_all(large, small):
+    rows = sum(PIECES)
+    vmem = pl.BlockSpec(memory_space=pltpu.VMEM)
+    landing = rows * 15 // 16
+    copies = 7 + len(PIECES) * Summed.COPIES
+    return pl.pallas_call(
+        sum_kernel,
+        out_shape=(
+            jax.ShapeDtypeStruct((2, rows, 256), LOW),
+            jax.ShapeDtypeStruct(small.shape, jnp.float32),
+        ),
+        in_specs=[vmem, vmem],
+        out_specs=(vmem, vmem),
+        scratch_shapes=[
+            pltpu.VMEM((rows, 256), LOW),
+            pltpu.VMEM((landing, 256), LOW),
+            pltpu.VMEM((2, rows, 256), LOW),
+            pltpu.VMEM((rows, 256), LOW),
+            pltpu.VMEM((7,) + small.shape, jnp.float32),
+            pltpu.SemaphoreType.DMA((copies,)),
+            pltpu.SemaphoreType.DMA((copies,)),
+        ],
+        compiler_params=pltpu.CompilerParams(
+            collective_id=0, has_side_effects=True, vmem_limit_bytes=56 << 20
+        ),
+    )(large, small)
+
+
+def halves(grad):
+    rows, columns = grad.shape
+    blocks = grad.astype(LOW).reshape(rows, 2, columns // 512, 256)
+    return blocks.transpose(1, 2, 0, 3).reshape(2, rows * columns // 512, 256)
+
+
+def whole(block, rows, columns):
+    wide = block.reshape(2, columns // 512, rows, 256).transpose(2, 0, 1, 3)
+    return wide.reshape(rows, columns).astype(jnp.float32)
+
+
+def sum_grads(grads):
+    large = [grad for grad in grads if grad.ndim == 2]
+    small = jnp.stack([grad for grad in grads if grad.ndim == 1] + [jnp.zeros((512,), jnp.float32)] * 2)
+    done, small = sum_all(jnp.concatenate([halves(grad) for grad in large], axis=1), small)
+    at, number, summed = 0, 0, []
+    for grad in grads:
+        if grad.ndim == 1:
+            summed.append(small[number])
+            number += 1
+        else:
+            size = grad.size // 512
+            summed.append(whole(done[:, at : at + size], *grad.shape))
+            at += size
+    return summed
 
 
 def layer_norm(hidden, gain, shift):
@@ -33,7 +317,12 @@
     )
 
 
+def sum_plain(grads):
+    return lax.psum(grads, ("rows", "seq"))
+
+
 def body(
+    sum_over_devices,
     states,
     memory,
     target_segments,
@@ -354,7 +643,7 @@
         + backward_dot(grad_k, self_key)
         + backward_dot(grad_v, self_value)
     )[None]
-    summed = lax.psum(
+    summed = sum_over_devices(
         (
             self_query_grad,
             self_key_grad,
@@ -372,8 +661,7 @@
             reduce_weight_grad,
             gain_three_grad,
             shift_three_grad,
-        ),
-        ("rows", "seq"),
+        )
     )
     (
         self_query_grad,
@@ -416,8 +704,9 @@
 
 
 def solution(mesh):
+    fast = dict(mesh.shape) == {"rows": 2, "seq": 16}
     return jax.shard_map(
-        body,
+        functools.partial(body, sum_grads if fast else sum_plain),
         mesh=mesh,
         in_specs=(
             P("rows", "seq", None),

time: 864 us -> 775 us (0.90)
  waiting for transfers between devices: 333 us -> 68.8 us
  Pallas kernels: 0 us -> 168 us
  blocking collectives: 193 us -> 110 us
  local copies, waits for them, and re-layouts: 102 us -> 177 us
  other arithmetic: 24.6 us -> 34.2 us
    psum x1 -> x0, waiting for transfers between devices: 249 us -> none  [body(): lax.psum((self_query_grad, self_key_grad, self_value_grad, self_out_grad,...]
    pallas_call x0 -> x1, Pallas kernels: none -> 168 us  [sum_all(): pl.pallas_call(sum_kernel, out_shape=(jax.ShapeDtypeStruct((2, rows, 256)...]
    psum x1 -> x0, blocking collectives: 82.9 us -> none  [body(): lax.psum((self_query_grad, self_key_grad, self_value_grad, self_out_grad,...]
    convert_element_type x0 -> x11, local copies, waits for them, and re-layouts: none -> 34.9 us  [whole(): return wide.reshape(rows, columns).astype(jnp.float32)]
    unnamed x166 -> x162, local copies, waits for them, and re-layouts: 36.2 us -> 54.9 us
    reshape x0 -> x11, local copies, waits for them, and re-layouts: none -> 18.6 us  [halves(): blocks = grad.astype(LOW).reshape(rows, 2, columns // 512, 256)]
    unnamed x9 -> x8, waiting for transfers between devices: 43.8 us -> 30.9 us
    convert_element_type x0 -> x3, other arithmetic: none -> 8.87 us  [whole(): return wide.reshape(rows, columns).astype(jnp.float32)]
  transfers between devices with their start and end apart: 7 -> 6, of which waited for: 4 -> 3; matrix products, arithmetic and copies ran while one was open for 12% -> 15% of each run, Pallas kernels for 0% -> 0%
where the time goes in v1:
time: 775 us; the launch traced here: 763 us
  local copies, waits for them, and re-layouts  177 us (23%)
  Pallas kernels  168 us (22%)
  matrix products  142 us (18%)
  blocking collectives  110 us (14%)
  waiting for transfers between devices  68.8 us (9%)
  loops' own time  43.7 us (6%)
  other arithmetic  34.2 us (4%)
  between operations  19.3 us (2%)
    pallas_call x1, Pallas kernels, sum_all(): pl.pallas_call(sum_kernel, out_shape=(jax.ShapeDtypeStruct((2, rows, 256)...  168 us
    unnamed x162, local copies, waits for them, and re-layouts  54.9 us
    another operation x1, loops' own time, both_sides(): return lax.fori_loop(0, shards, one_shard, grads)  42 us
    all_gather x1, waiting for transfers between devices, body(): lax.all_gather(d_attended, 'seq', axis=0, tiled=True)  36.4 us
    convert_element_type x11, local copies, waits for them, and re-layouts, whole(): return wide.reshape(rows, columns).astype(jnp.float32)  34.9 us
    dot_general x16, matrix products, key_part(): jnp.einsum('qhk,qhd->khd', grads_s, piece_query_heads, preferred_element_...  33.6 us
    unnamed x8, waiting for transfers between devices  30.9 us
    dot_general x16, matrix products, key_part(): jnp.einsum('qhk,qhd->khd', probs.astype(low_type), piece_grad_heads, pref...  28.9 us
  transfers between devices with their start and end apart: 6, of which 3 were waited for; matrix products, arithmetic and copies ran while one was open for 15% of the time, Pallas kernels for 0%

profile of v1, /device:TPU:0, one launch (start us, length us, event | category | flops | bytes accessed | tf_op | source)
XLA Modules:
  0.0 762.7 jit_solution(11358585061876869283)
XLA Ops:
  13.6 23.8 %all-gather = s32[1,2048]{1,0:T(1,128)} all-gather(s32[1,128]{1,0:T(1,128)} %param.30), channel_id=2, replica_groups=mesh['rows'=2,'seq'=16] {'seq'}, dimensions={1}, use_global_device_ids=true | all-gather | bytes 8704 | tf_op jit(solution)/shard_map/all_gather | solution.py:370
  41.0 17.9 %all_gather.36 = bf16[128,512]{1,0:T(8,128)(2,1)S(1)} all-gather(bf16[8,512]{1,0:T(8,128)(2,1)S(1)} %convolution_convert_fusion.18), channel_id=1, replica_groups=mesh['rows'=2,'seq'=16] {'seq'}, dimensions={0}, use_global_device_ids=true | all-gather | bytes 139264 | tf_op jit(solution)/shard_map/all_gather | solution.py:421
  60.9 19.1 %all_gather.38 = bf16[128,512]{1,0:T(8,128)(2,1)S(1)} all-gather(bf16[8,512]{1,0:T(8,128)(2,1)S(1)} %convolution_convert_fusion.17), channel_id=1, replica_groups=mesh['rows'=2,'seq'=16] {'seq'}, dimensions={0}, use_global_device_ids=true | all-gather | bytes 139264 | tf_op jit(solution)/shard_map/all_gather | solution.py:420
  87.2 8.2 %all-reduce = s32[128]{0:T(128)S(1)} all-reduce(s32[128]{0:T(128)S(1)} %bitcast_dynamic-update-slice_fusion.9), channel_id=3, replica_groups=mesh['rows'=2,'seq'=16] {'seq'}, use_global_device_ids=true, to_apply=%add | all-reduce | flops 128 | bytes 1024
  97.7 24.6 %conditional.2 = (f32[128,8]{0,1:T(8,128)S(1)}, f32[128,8]{0,1:T(8,128)S(1)}, f32[128,8,64]{0,2,1:T(8,128)S(1)}, f32[128,8]{0,1:T(8,128)}) conditional(s32[]{:T(128)} %convert_element_type.305, (s32[1,128]{1,0:T(1,128)S(1)}, s32[2048]{0:T(1024)}, s32[2048]{0:T(1024)S(1)}, s32[128]{0:T(128)S(1)}, bf16[2048,512]{1,0:T(8,128)(2,1)}, ...), branch_computations={%region_0.3_spmd, %region_3.4_spmd} | conditional | flops 564919296 | bytes 72795200 | solution.py:405
  190.2 21.7 %all_gather.40 = f32[2048,8]{0,1:T(8,128)} all-gather(f32[128,8]{0,1:T(8,128)} %add.191), channel_id=1, replica_groups=mesh['rows'=2,'seq'=16] {'seq'}, dimensions={0}, use_global_device_ids=true | all-gather | bytes 69632 | tf_op jit(solution)/shard_map/all_gather | solution.py:503
  211.8 19.2 %all_gather.42 = f32[2048,8]{0,1:T(8,128)} all-gather(f32[128,8]{0,1:T(8,128)S(1)} %multiply_reduce_fusion.3), channel_id=1, replica_groups=mesh['rows'=2,'seq'=16] {'seq'}, dimensions={0}, use_global_device_ids=true | all-gather | bytes 69632 | tf_op jit(solution)/shard_map/all_gather | solution.py:504
  235.2 30.8 %reduce-scatter.9.cloned.1.call-done = f32[8,512]{1,0:T(8,128)} async-done(((f32[128,512]{1,0:T(8,128)}), f32[8,512]{1,0:T(8,128)}) %reduce-scatter.9.cloned.1.call-update) | async-done | bytes 16400
  272.0 36.4 %all-gather.13.cloned.1.call-done = bf16[2048,512]{1,0:T(8,128)(2,1)} async-done(((bf16[128,512]{1,0:T(8,128)(2,1)}), bf16[2048,512]{1,0:T(8,128)(2,1)}) %all-gather.13.cloned.1.call-update) | async-done | bytes 2097168 | tf_op jit(solution)/shard_map/all_gather | solution.py:630
  312.3 180.5 %while.19 = (s32[]{:T(128)}, f32[128,8,64]{2,1,0:T(8,128)S(1)}, f32[128,8,64]{0,2,1:T(8,128)}, f32[128,8,64]{0,2,1:T(8,128)}, s32[2048]{0:T(1024)}, /*index=5*/s...) while((s32[]{:T(128)}, f32[128,8,64]{2,1,0:T(8,128)S(1)}, ...), condition=%wide.region_24.25_spmd.clone.clone, body=%wide.region_20.24_spmd.clone.clone.sunk | while | flops 68403480 | bytes 12235485 | solution.py:622
  320.3 7.8 %conditional.6 = ((f32[128,8,64]{2,1,0:T(8,128)S(1)}, f32[128,8,64]{0,2,1:T(8,128)}, f32[128,8,64]{0,2,1:T(8,128)})) conditional(s32[]{:T(128)} %clamp.10, (f32[128,8,64]{2,1,0:T(8,128)S(1)}, f32[128,8,64]{0,2,1:T(8,128)}, f32[128,8,64]{0,2,1:T(8,128)}) %tuple.128, (s32[]{:T(128)}, bf16[2048,512]{1,0:T(8,128)(2,1)S(1)}, ...), branch_computations={%region_21.21_spmd, %region_22.22_spmd, %region_23.23_spmd} | conditional | flops 68403336 | bytes 12233302 | solution.py:620
  332.1 7.8 %conditional.6 = ((f32[128,8,64]{2,1,0:T(8,128)S(1)}, f32[128,8,64]{0,2,1:T(8,128)}, f32[128,8,64]{0,2,1:T(8,128)})) conditional(s32[]{:T(128)} %clamp.10, (f32[128,8,64]{2,1,0:T(8,128)S(1)}, f32[128,8,64]{0,2,1:T(8,128)}, f32[128,8,64]{0,2,1:T(8,128)}) %tuple.128, (s32[]{:T(128)}, bf16[2048,512]{1,0:T(8,128)(2,1)S(1)}, ...), branch_computations={%region_21.21_spmd, %region_22.22_spmd, %region_23.23_spmd} | conditional | flops 68403336 | bytes 12233302 | solution.py:620
  343.9 7.8 %conditional.6 = ((f32[128,8,64]{2,1,0:T(8,128)S(1)}, f32[128,8,64]{0,2,1:T(8,128)}, f32[128,8,64]{0,2,1:T(8,128)})) conditional(s32[]{:T(128)} %clamp.10, (f32[128,8,64]{2,1,0:T(8,128)S(1)}, f32[128,8,64]{0,2,1:T(8,128)}, f32[128,8,64]{0,2,1:T(8,128)}) %tuple.128, (s32[]{:T(128)}, bf16[2048,512]{1,0:T(8,128)(2,1)S(1)}, ...), branch_computations={%region_21.21_spmd, %region_22.22_spmd, %region_23.23_spmd} | conditional | flops 68403336 | bytes 12233302 | solution.py:620
  367.4 7.8 %conditional.6 = ((f32[128,8,64]{2,1,0:T(8,128)S(1)}, f32[128,8,64]{0,2,1:T(8,128)}, f32[128,8,64]{0,2,1:T(8,128)})) conditional(s32[]{:T(128)} %clamp.10, (f32[128,8,64]{2,1,0:T(8,128)S(1)}, f32[128,8,64]{0,2,1:T(8,128)}, f32[128,8,64]{0,2,1:T(8,128)}) %tuple.128, (s32[]{:T(128)}, bf16[2048,512]{1,0:T(8,128)(2,1)S(1)}, ...), branch_computations={%region_21.21_spmd, %region_22.22_spmd, %region_23.23_spmd} | conditional | flops 68403336 | bytes 12233302 | solution.py:620
  390.9 7.8 %conditional.6 = ((f32[128,8,64]{2,1,0:T(8,128)S(1)}, f32[128,8,64]{0,2,1:T(8,128)}, f32[128,8,64]{0,2,1:T(8,128)})) conditional(s32[]{:T(128)} %clamp.10, (f32[128,8,64]{2,1,0:T(8,128)S(1)}, f32[128,8,64]{0,2,1:T(8,128)}, f32[128,8,64]{0,2,1:T(8,128)}) %tuple.128, (s32[]{:T(128)}, bf16[2048,512]{1,0:T(8,128)(2,1)S(1)}, ...), branch_computations={%region_21.21_spmd, %region_22.22_spmd, %region_23.23_spmd} | conditional | flops 68403336 | bytes 12233302 | solution.py:620
  402.7 7.8 %conditional.6 = ((f32[128,8,64]{2,1,0:T(8,128)S(1)}, f32[128,8,64]{0,2,1:T(8,128)}, f32[128,8,64]{0,2,1:T(8,128)})) conditional(s32[]{:T(128)} %clamp.10, (f32[128,8,64]{2,1,0:T(8,128)S(1)}, f32[128,8,64]{0,2,1:T(8,128)}, f32[128,8,64]{0,2,1:T(8,128)}) %tuple.128, (s32[]{:T(128)}, bf16[2048,512]{1,0:T(8,128)(2,1)S(1)}, ...), branch_computations={%region_21.21_spmd, %region_22.22_spmd, %region_23.23_spmd} | conditional | flops 68403336 | bytes 12233302 | solution.py:620
  414.4 7.8 %conditional.6 = ((f32[128,8,64]{2,1,0:T(8,128)S(1)}, f32[128,8,64]{0,2,1:T(8,128)}, f32[128,8,64]{0,2,1:T(8,128)})) conditional(s32[]{:T(128)} %clamp.10, (f32[128,8,64]{2,1,0:T(8,128)S(1)}, f32[128,8,64]{0,2,1:T(8,128)}, f32[128,8,64]{0,2,1:T(8,128)}) %tuple.128, (s32[]{:T(128)}, bf16[2048,512]{1,0:T(8,128)(2,1)S(1)}, ...), branch_computations={%region_21.21_spmd, %region_22.22_spmd, %region_23.23_spmd} | conditional | flops 68403336 | bytes 12233302 | solution.py:620
  426.2 7.8 %conditional.6 = ((f32[128,8,64]{2,1,0:T(8,128)S(1)}, f32[128,8,64]{0,2,1:T(8,128)}, f32[128,8,64]{0,2,1:T(8,128)})) conditional(s32[]{:T(128)} %clamp.10, (f32[128,8,64]{2,1,0:T(8,128)S(1)}, f32[128,8,64]{0,2,1:T(8,128)}, f32[128,8,64]{0,2,1:T(8,128)}) %tuple.128, (s32[]{:T(128)}, bf16[2048,512]{1,0:T(8,128)(2,1)S(1)}, ...), branch_computations={%region_21.21_spmd, %region_22.22_spmd, %region_23.23_spmd} | conditional | flops 68403336 | bytes 12233302 | solution.py:620
  438.0 7.8 %conditional.6 = ((f32[128,8,64]{2,1,0:T(8,128)S(1)}, f32[128,8,64]{0,2,1:T(8,128)}, f32[128,8,64]{0,2,1:T(8,128)})) conditional(s32[]{:T(128)} %clamp.10, (f32[128,8,64]{2,1,0:T(8,128)S(1)}, f32[128,8,64]{0,2,1:T(8,128)}, f32[128,8,64]{0,2,1:T(8,128)}) %tuple.128, (s32[]{:T(128)}, bf16[2048,512]{1,0:T(8,128)(2,1)S(1)}, ...), branch_computations={%region_21.21_spmd, %region_22.22_spmd, %region_23.23_spmd} | conditional | flops 68403336 | bytes 12233302 | solution.py:620
  449.8 7.8 %conditional.6 = ((f32[128,8,64]{2,1,0:T(8,128)S(1)}, f32[128,8,64]{0,2,1:T(8,128)}, f32[128,8,64]{0,2,1:T(8,128)})) conditional(s32[]{:T(128)} %clamp.10, (f32[128,8,64]{2,1,0:T(8,128)S(1)}, f32[128,8,64]{0,2,1:T(8,128)}, f32[128,8,64]{0,2,1:T(8,128)}) %tuple.128, (s32[]{:T(128)}, bf16[2048,512]{1,0:T(8,128)(2,1)S(1)}, ...), branch_computations={%region_21.21_spmd, %region_22.22_spmd, %region_23.23_spmd} | conditional | flops 68403336 | bytes 12233302 | solution.py:620
  461.5 7.8 %conditional.6 = ((f32[128,8,64]{2,1,0:T(8,128)S(1)}, f32[128,8,64]{0,2,1:T(8,128)}, f32[128,8,64]{0,2,1:T(8,128)})) conditional(s32[]{:T(128)} %clamp.10, (f32[128,8,64]{2,1,0:T(8,128)S(1)}, f32[128,8,64]{0,2,1:T(8,128)}, f32[128,8,64]{0,2,1:T(8,128)}) %tuple.128, (s32[]{:T(128)}, bf16[2048,512]{1,0:T(8,128)(2,1)S(1)}, ...), branch_computations={%region_21.21_spmd, %region_22.22_spmd, %region_23.23_spmd} | conditional | flops 68403336 | bytes 12233302 | solution.py:620
  473.3 7.8 %conditional.6 = ((f32[128,8,64]{2,1,0:T(8,128)S(1)}, f32[128,8,64]{0,2,1:T(8,128)}, f32[128,8,64]{0,2,1:T(8,128)})) conditional(s32[]{:T(128)} %clamp.10, (f32[128,8,64]{2,1,0:T(8,128)S(1)}, f32[128,8,64]{0,2,1:T(8,128)}, f32[128,8,64]{0,2,1:T(8,128)}) %tuple.128, (s32[]{:T(128)}, bf16[2048,512]{1,0:T(8,128)(2,1)S(1)}, ...), branch_computations={%region_21.21_spmd, %region_22.22_spmd, %region_23.23_spmd} | conditional | flops 68403336 | bytes 12233302 | solution.py:620
  485.0 7.8 %conditional.6 = ((f32[128,8,64]{2,1,0:T(8,128)S(1)}, f32[128,8,64]{0,2,1:T(8,128)}, f32[128,8,64]{0,2,1:T(8,128)})) conditional(s32[]{:T(128)} %clamp.10, (f32[128,8,64]{2,1,0:T(8,128)S(1)}, f32[128,8,64]{0,2,1:T(8,128)}, f32[128,8,64]{0,2,1:T(8,128)}) %tuple.128, (s32[]{:T(128)}, bf16[2048,512]{1,0:T(8,128)(2,1)S(1)}, ...), branch_computations={%region_21.21_spmd, %region_22.22_spmd, %region_23.23_spmd} | conditional | flops 68403336 | bytes 12233302 | solution.py:620
  515.2 167.8 %shard_map.348 = (bf16[2,8192,256]{2,1,0:T(8,128)(2,1)}, f32[8,512]{1,0:T(8,128)}) custom-call(bf16[2,8192,256]{2,1,0:T(8,128)(2,1)} %bitcast_dynamic-update-slice_fusion.given, f32[8,512]{1,0:T(8,128)} %stack.5.small), custom_call_target="tpu_custom_call" | custom-call | tf_op jit(solution)/shard_map/pallas_call | solution.py:244
  (485 shorter events, 370.5 us)
Async XLA Ops:
  7.2 128.4 %copy-start = (bf16[512,2048]{1,0:T(8,128)(2,1)S(1)}, bf16[512,2048]{1,0:T(8,128)(2,1)}, u32[]{:S(2)}) copy-start(bf16[512,2048]{1,0:T(8,128)(2,1)} %param.44) | copy-start | bytes 6291460
  7.2 78.6 %copy-start.67 = (u32[32]{0:T(128)S(1)}, u32[32]{0:T(128)}, u32[]{:S(2)}) copy-start(u32[32]{0:T(128)} %constant.124) | copy-start | bytes 388
  7.2 88.2 %copy-start.40 = (s32[1,128]{1,0:T(1,128)S(1)}, s32[1,128]{1,0:T(1,128)}, u32[]{:S(2)}) copy-start(s32[1,128]{1,0:T(1,128)} %param.30) | copy-start | bytes 1540
  7.2 79.9 %copy-start.66 = (s32[1,8]{1,0:T(1,128)S(1)}, s32[1,8]{1,0:T(1,128)}, u32[]{:S(2)}) copy-start(s32[1,8]{1,0:T(1,128)} %param.31) | copy-start | bytes 100
  7.2 88.9 %all-gather.7.cloned.1.call-start = ((), (), s32[]{:S(2)}) async-start(), calls=%async_computation.2 | async-start | bytes 2228224 | tf_op jit(solution)/shard_map/all_gather | solution.py:368
  9.4 88.2 %all-gather.9.cloned.1.call-start = ((), (), s32[]{:S(2)}) async-start(), calls=%async_computation.3 | async-start | bytes 2228224 | tf_op jit(solution)/shard_map/all_gather | solution.py:369
  11.5 174.7 %all-gather.11.cloned.1.call-start = ((), (), s32[]{:S(2)}) async-start(), calls=%async_computation.4 | async-start | bytes 2228224 | tf_op jit(solution)/shard_map/all_gather | solution.py:629
  13.6 219.4 %reduce-scatter.7.cloned.1.call-start = ((), (), s32[]{:S(2)}) async-start(), calls=%async_computation.6 | async-start | bytes 278528
  97.7 24.7 %copy-start.7 = (bf16[1,128,512]{2,1,0:T(8,128)(2,1)S(1)}, bf16[1,128,512]{2,1,0:T(8,128)(2,1)}, u32[]{:S(2)}) copy-start(bf16[1,128,512]{2,1,0:T(8,128)(2,1)} %param.28) | copy-start | bytes 393220
  97.7 27.6 %copy-start.43 = (f32[512]{0:T(512)S(1)}, f32[512]{0:T(512)}, u32[]{:S(2)}) copy-start(f32[512]{0:T(512)} %param.36) | copy-start | bytes 6148
  122.3 11.6 %copy-start.31 = (f32[128,8,64]{0,2,1:T(8,128)}, f32[128,8,64]{0,2,1:T(8,128)S(1)}, u32[]{:S(2)}) copy-start(f32[128,8,64]{0,2,1:T(8,128)S(1)} %get-tuple-element.482) | copy-start | bytes 786436
  122.3 11.6 %copy-start.11 = (bf16[512,512]{1,0:T(8,128)(2,1)S(1)}, bf16[512,512]{1,0:T(8,128)(2,1)}, u32[]{:S(2)}) copy-start(bf16[512,512]{1,0:T(8,128)(2,1)} %param.41) | copy-start | bytes 1572868
  122.4 13.1 %copy-start.27 = (bf16[128,8,64]{0,2,1:T(8,128)(2,1)}, bf16[128,8,64]{0,2,1:T(8,128)(2,1)S(1)}, u32[]{:S(2)}) copy-start(bf16[128,8,64]{0,2,1:T(8,128)(2,1)S(1)} %fusion.84) | copy-start | bytes 393220
  147.5 13.7 %copy-start.32 = (f32[128,8,64]{0,2,1:T(8,128)S(1)}, f32[128,8,64]{0,2,1:T(8,128)}, u32[]{:S(2)}) copy-start(f32[128,8,64]{0,2,1:T(8,128)} %copy-done.31) | copy-start | bytes 786436
  152.7 12.1 %copy-start.28 = (bf16[128,8,64]{0,2,1:T(8,128)(2,1)S(1)}, bf16[128,8,64]{0,2,1:T(8,128)(2,1)}, u32[]{:S(2)}) copy-start(bf16[128,8,64]{0,2,1:T(8,128)(2,1)} %copy-done.27) | copy-start | bytes 393220
  152.7 113.3 %reduce-scatter.9.cloned.1.call-start = ((), (), s32[]{:S(2)}) async-start(), calls=%async_computation.7 | async-start | bytes 278528
  154.2 12.6 %copy-start.8 = (f32[128,512]{1,0:T(8,128)}, f32[128,512]{1,0:T(8,128)S(1)}, u32[]{:S(2)}) copy-start(f32[128,512]{1,0:T(8,128)S(1)} %get-tuple-element.805) | copy-start | bytes 786436
  154.3 154.2 %all-gather.13.cloned.1.call-start = ((), (), s32[]{:S(2)}) async-start(), calls=%async_computation.5 | async-start | bytes 2228224 | tf_op jit(solution)/shard_map/all_gather | solution.py:630
  181.5 49.5 %copy-start.10 = (bf16[128,8,128]{0,2,1:T(8,128)(2,1)S(1)}, bf16[128,8,128]{0,2,1:T(8,128)(2,1)}, u32[]{:S(2)}) copy-start(bf16[128,8,128]{0,2,1:T(8,128)(2,1)} %copy-done.9) | copy-start | bytes 786436
  181.5 50.5 %copy-start.14 = (f32[128,8,128]{0,2,1:T(8,128)S(1)}, f32[128,8,128]{0,2,1:T(8,128)}, u32[]{:S(2)}) copy-start(f32[128,8,128]{0,2,1:T(8,128)} %copy-done.13) | copy-start | bytes 1572868
  181.5 52.3 %copy-start.41 = (bf16[1,8,512]{2,1,0:T(8,128)(2,1)S(1)}, bf16[1,8,512]{2,1,0:T(8,128)(2,1)}, u32[]{:S(2)}) copy-start(bf16[1,8,512]{2,1,0:T(8,128)(2,1)} %param.29) | copy-start | bytes 24580
  234.2 78.2 %copy-start.2 = (bf16[2048,512]{1,0:T(8,128)(2,1)S(1)}, bf16[2048,512]{1,0:T(8,128)(2,1)}, u32[]{:S(2)}) copy-start(bf16[2048,512]{1,0:T(8,128)(2,1)} %all-gather.7.cloned.1.call-done) | copy-start | bytes 6291460
  499.8 11.6 %copy-start.19 = (bf16[512,2,1,256]{3,0,1,2:T(8,128)(2,1)S(1)}, bf16[512,2,1,256]{3,0,1,2:T(8,128)(2,1)}, u32[]{:S(2)}) copy-start(bf16[512,2,1,256]{3,0,1,2:T(8,128)(2,1)} %copy.175) | copy-start | bytes 1572868
  500.9 11.3 %copy-start.5 = (bf16[512,2,4,256]{3,0,2,1:T(8,128)(2,1)S(1)}, bf16[512,2,4,256]{3,0,2,1:T(8,128)(2,1)}, u32[]{:S(2)}) copy-start(bf16[512,2,4,256]{3,0,2,1:T(8,128)(2,1)} %copy.176) | copy-start | bytes 6291460
  (64 other events, 255.9 us)
Sparse Core Ops, SparseCore 0:
  10.8 44.4 all-gather.6
  57.5 40.1 all-gather.8
  99.8 40.3 all-gather.10
  152.8 54.7 reduce-scatter.6
  211.6 54.3 reduce-scatter.8
  268.0 40.4 all-gather.12

commit v2 on v0

--- a/solution.py
+++ b/solution.py
@@ -1,10 +1,19 @@
+import inspect
+import math
+import types
+
 import jax
 import jax.numpy as jnp
 from jax import lax
+from jax.experimental import pallas as pl
+from jax.experimental.pallas import tpu as pltpu
 from jax.sharding import PartitionSpec as P
 
 HEADS = 8
 HEAD_DIM = 64
+MESH = pl.DeviceIdType.MESH
+LOW = jnp.bfloat16
+ROWS, SEQ = "rows", "seq"
 
 
 def layer_norm(hidden, gain, shift):
@@ -63,7 +72,7 @@
     query_seg = target_segments[0]
     memory_seg = memory_segments[0]
     count = tokens.shape[0]
-    own_start = lax.axis_index("seq") * count
+    own_start = lax.axis_index(SEQ) * count
     query_pos = own_start + jnp.arange(count, dtype=jnp.int32)
     queries = forward_dot(tokens, self_query).astype(low_type)
     keys = forward_dot(tokens, self_key).astype(low_type)
@@ -76,9 +85,9 @@
         jnp.zeros((count, HEADS), jnp.float32),
         jnp.zeros((count, HEADS, HEAD_DIM), jnp.float32),
     )
-    piece_keys = lax.all_gather(keys, "seq", axis=0, tiled=True)
-    piece_values = lax.all_gather(values, "seq", axis=0, tiled=True)
-    piece_seg = lax.all_gather(query_seg, "seq", axis=0, tiled=True)
+    piece_keys = lax.all_gather(keys, SEQ, axis=0, tiled=True)
+    piece_values = lax.all_gather(values, SEQ, axis=0, tiled=True)
+    piece_seg = lax.all_gather(query_seg, SEQ, axis=0, tiled=True)
     width = piece_keys.shape[0]
     key_pos = jnp.arange(width, dtype=jnp.int32)
     skip = (
@@ -128,9 +137,9 @@
     memory_keys = forward_dot(local_memory, cross_key).astype(low_type)
     memory_values = forward_dot(local_memory, cross_value).astype(low_type)
     all_keys, all_values, all_seg = (
-        lax.all_gather(memory_keys, "seq", axis=0, tiled=True),
-        lax.all_gather(memory_values, "seq", axis=0, tiled=True),
-        lax.all_gather(memory_seg, "seq", axis=0, tiled=True),
+        lax.all_gather(memory_keys, SEQ, axis=0, tiled=True),
+        lax.all_gather(memory_values, SEQ, axis=0, tiled=True),
+        lax.all_gather(memory_seg, SEQ, axis=0, tiled=True),
     )
     cross_heads = split_heads(cross_q)
     mem_key_heads = split_heads(all_keys)
@@ -192,8 +201,8 @@
         "qhk,qhd->khd", cross_probs_low, d_crossed, preferred_element_type=jnp.float32
     ).reshape(-1, HEADS * HEAD_DIM)
     d_mem_keys, d_mem_values = (
-        lax.psum_scatter(key_terms, "seq", scatter_dimension=0, tiled=True),
-        lax.psum_scatter(value_terms, "seq", scatter_dimension=0, tiled=True),
+        lax.psum_scatter(key_terms, SEQ, scatter_dimension=0, tiled=True),
+        lax.psum_scatter(value_terms, SEQ, scatter_dimension=0, tiled=True),
     )
     d_mem_keys = d_mem_keys.astype(low_type)
     d_mem_values = d_mem_values.astype(low_type)
@@ -211,8 +220,8 @@
     d_heads = split_heads(d_attended)
     delta = jnp.sum(d_heads.astype(jnp.float32) * attended, axis=2)
     all_log, all_delta = (
-        lax.all_gather(log_total, "seq", axis=0, tiled=True),
-        lax.all_gather(delta, "seq", axis=0, tiled=True),
+        lax.all_gather(log_total, SEQ, axis=0, tiled=True),
+        lax.all_gather(delta, SEQ, axis=0, tiled=True),
     )
 
     def query_part(total_q, piece_keys, piece_values, piece_seg, start):
@@ -335,11 +344,11 @@
     grad_q, grad_k, grad_v = both_sides(
         (own_q, own_k, own_v),
         (
-            lax.all_gather(keys, "seq", axis=0, tiled=True),
-            lax.all_gather(values, "seq", axis=0, tiled=True),
-            lax.all_gather(queries, "seq", axis=0, tiled=True),
-            lax.all_gather(d_attended, "seq", axis=0, tiled=True),
-            lax.all_gather(query_seg, "seq", axis=0, tiled=True),
+            lax.all_gather(keys, SEQ, axis=0, tiled=True),
+            lax.all_gather(values, SEQ, axis=0, tiled=True),
+            lax.all_gather(queries, SEQ, axis=0, tiled=True),
+            lax.all_gather(d_attended, SEQ, axis=0, tiled=True),
+            lax.all_gather(query_seg, SEQ, axis=0, tiled=True),
         ),
     )
     grad_q = grad_q.reshape(count, HEADS * HEAD_DIM).astype(low_type)
@@ -373,7 +382,7 @@
             gain_three_grad,
             shift_three_grad,
         ),
-        ("rows", "seq"),
+        (ROWS, SEQ),
     )
     (
         self_query_grad,
@@ -415,37 +424,963 @@
     )
 
 
+EXTENT = {"x": 2, "y": 2, "z": 4}
+ORDERS = (("x", "y", "z"), ("y", "x", "z"))
+CHIPS = 8
+TOKENS = 128
+MODEL = 512
+HIDDEN = 2048
+SLOTS = 8
+AT = types.SimpleNamespace(
+    reduce=0,
+    expand=2048,
+    cross_out=4096,
+    memory=4608,
+    cross_query=5120,
+    self_out=5632,
+    self_query=6144,
+    self_key=6656,
+    self_value=7168,
+    cross_key=7680,
+    cross_value=8192,
+)
+SUMMED_ROWS = 7680
+DONE_ROWS = 8704
+PIECES = (1024, 1024, 1024, 1024, 1024, 1024, 1536)
+SEMAPHORES = 320
+
+
+def rows_at(start, size):
+    return pl.ds(pl.multiple_of(start, 16), size)
+
+
+def dot(left, right):
+    return jnp.dot(left, right, preferred_element_type=jnp.float32)
+
+
+def dot_rows(left, right):
+    return lax.dot_general(left, right, (((1,), (1,)), ((), ())), preferred_element_type=jnp.float32)
+
+
+def dot_tokens(left, right):
+    return lax.dot_general(left, right, (((0,), (0,)), ((), ())), preferred_element_type=jnp.float32)
+
+
+def left_lanes(rows):
+    return lax.broadcasted_iota(jnp.int32, (rows, 128), 1) < 64
+
+
+def turned(block):
+    return pltpu.roll(block, 64, 1)
+
+
+def fold_pair(block):
+    top, bottom, left = block[:64], block[64:], left_lanes(64)
+    return jnp.where(left, top, turned(bottom)), jnp.where(left, turned(top), bottom)
+
+
+def unfold_pair(even, odd):
+    left = left_lanes(64)
+    top = jnp.where(left, even, turned(odd))
+    bottom = jnp.where(left, turned(even), odd)
+    return jnp.concatenate([top, bottom], axis=0)
+
+
+class Place:
+    def __init__(self):
+        self.row = lax.axis_index(ROWS)
+        self.seq = lax.axis_index(SEQ)
+        self.core = lax.rem(self.seq, 2)
+        self.chip = self.seq // 2
+        self.at = {
+            "x": self.row,
+            "y": lax.rem(self.chip, 2),
+            "z": self.seq // 4,
+        }
+
+    def sibling(self):
+        return (self.row, self.seq + 1 - 2 * self.core)
+
+    def on_chip(self, chip):
+        return (self.row, 2 * chip + self.core)
+
+    def moved(self, dim, step):
+        there = lax.rem(self.at[dim] + step, EXTENT[dim])
+        if dim == "x":
+            return there, (there, self.seq)
+        weight = 2 if dim == "y" else 4
+        return there, (self.row, self.seq + (there - self.at[dim]) * weight)
+
+
+class Links:
+    def __init__(self, place, send, recv):
+        self.place, self.send, self.recv = place, send, recv
+        self.used = 0
+
+    def take(self, count):
+        first = self.used
+        self.used += count
+        assert self.used <= SEMAPHORES
+        return first
+
+    def copy(self, src, dst, device, sent, arrived):
+        return pltpu.make_async_remote_copy(
+            src_ref=src,
+            dst_ref=dst,
+            send_sem=self.send.at[sent],
+            recv_sem=self.recv.at[arrived],
+            device_id=device,
+            device_id_type=MESH,
+        )
+
+    def local(self, src, dst, arrived):
+        return pltpu.make_async_copy(src, dst, self.recv.at[arrived])
+
+
+class Spread:
+    def __init__(self, links, out, into):
+        self.links, self.out, self.into = links, out, into
+        self.base = links.take(CHIPS)
+        self.chip = links.place.chip
+
+    def _copy(self, there, sent):
+        return self.links.copy(
+            self.out.at[there],
+            self.into.at[self.chip],
+            self.links.place.on_chip(there),
+            self.base + sent,
+            self.base + self.chip,
+        )
+
+    def _own(self):
+        return self.links.local(self.out.at[self.chip], self.into.at[self.chip], self.base + self.chip)
+
+    def start_all(self):
+        for hop in range(1, CHIPS):
+            self._copy(lax.rem(self.chip + hop, CHIPS), hop).start()
+        self._own().start()
+
+    def end_all(self):
+        for hop in range(1, CHIPS):
+            self._copy(lax.rem(self.chip + hop, CHIPS), hop).wait_send()
+
+    def start(self, there):
+        @pl.when(self.chip != there)
+        def _():
+            self._copy(there, there).start()
+
+        @pl.when(self.chip == there)
+        def _():
+            self._own().start()
+
+    def end(self, there):
+        @pl.when(self.chip != there)
+        def _():
+            self._copy(there, there).wait_send()
+
+    def wait_from(self, chip):
+        self.links.local(self.into.at[chip], self.into.at[chip], self.base + chip).wait()
+
+
+class Pair:
+    def __init__(self, links, src, dst):
+        self.made = None
+        self.links, self.src, self.dst = links, src, dst
+        self.sem = links.take(1)
+
+    def _copy(self):
+        return self.links.copy(self.src, self.dst, self.links.place.sibling(), self.sem, self.sem)
+
+    def start(self):
+        self._copy().start()
+
+    def wait(self):
+        self._copy().wait()
+
+
+class Summed:
+    def __init__(self, links, part, landing, done, start, size, landing_at):
+        self.links, self.place = links, links.place
+        self.part, self.landing, self.done = part, landing, done
+        self.start, self.size = start, size
+        self.plan = []
+        half = size // 2
+        for color, order in enumerate(ORDERS):
+            steps, span = [], half
+            base = start + color * half
+            for dim in order:
+                extent = EXTENT[dim]
+                share = span // extent
+                own = base + self.place.at[dim] * share
+                sem = links.take(2 * (extent - 1))
+                steps.append((dim, base, share, own, landing_at, sem))
+                landing_at += share * (extent - 1)
+                base, span = own, share
+            self.plan.append(steps)
+        self.landing_end = landing_at
+        mine = done.at[self.place.core, pl.ds(start, size)]
+        self.across = Pair(links, mine, mine)
+
+    def _out(self, color, step):
+        dim, base, share, own, at, sem = self.plan[color][step]
+        copies = []
+        for hop in range(1, EXTENT[dim]):
+            there, device = self.place.moved(dim, hop)
+            src = self.part.at[rows_at(base + there * share, share)]
+            dst = self.landing.at[pl.ds(at + (hop - 1) * share, share)]
+            copies.append(self.links.copy(src, dst, device, sem + hop - 1, sem + hop - 1))
+        return copies
+
+    def _back(self, color, step):
+        dim, base, share, own, at, sem = self.plan[color][step]
+        sem = sem + EXTENT[dim] - 1
+        mine = self.done.at[self.place.core, rows_at(own, share)]
+        copies = []
+        for hop in range(1, EXTENT[dim]):
+            device = self.place.moved(dim, hop)[1]
+            copies.append(self.links.copy(mine, mine, device, sem + hop - 1, sem + hop - 1))
+        return copies
+
+    def begin(self):
+        for color in range(2):
+            for copy in self._out(color, 0):
+                copy.start()
+
+    def gather(self, step):
+        for color in range(2):
+            dim, base, share, own, at, sem = self.plan[color][step]
+            for copy in self._out(color, step):
+                copy.wait()
+            block = math.gcd(share, 128)
+
+            def add(number, carry, step=step, share=share, own=own, at=at, dim=dim, block=block):
+                rows = rows_at(own + number * block, block)
+                total = self.part[rows].astype(jnp.float32)
+                for hop in range(1, EXTENT[dim]):
+                    here = rows_at(at + (hop - 1) * share + number * block, block)
+                    total = total + self.landing[here].astype(jnp.float32)
+                if step == 2:
+                    self.done[self.place.core, rows] = total.astype(LOW)
+                else:
+                    self.part[rows] = total.astype(LOW)
+                return carry
+
+            lax.fori_loop(0, share // block, add, 0)
+            for copy in self._out(color, step + 1) if step < 2 else self._back(color, 2):
+                copy.start()
+
+    def spread(self, step):
+        for color in range(2):
+            for copy in self._back(color, step):
+                copy.wait()
+            if step > 0:
+                for copy in self._back(color, step - 1):
+                    copy.start()
+        if step == 0:
+            self.across.start()
+
+    def advance(self, event):
+        if event < 3:
+            self.gather(event)
+        elif event < 6:
+            self.spread(5 - event)
+        else:
+            self.across.wait()
+
+
+class Rows:
+    def __init__(self, links, held, landing):
+        self.links, self.place = links, links.place
+        self.held, self.landing = held, landing
+        self.base = links.take(6)
+
+    def _copies(self, step):
+        if step < 3:
+            device = self.place.sibling() if step == 0 else self.place.moved("xy"[step - 1], 1)[1]
+            return [self.links.copy(self.held, self.landing.at[step], device, self.base + step, self.base + step)]
+        here = self.landing.at[3 + self.place.at["z"]]
+        sem = self.base + 2
+        return [
+            self.links.copy(self.held, here, self.place.moved("z", hop)[1], sem + hop, sem + hop)
+            for hop in (1, 2, 3)
+        ]
+
+    def begin(self):
+        for copy in self._copies(0):
+            copy.start()
+
+    def advance(self, event):
+        for copy in self._copies(event):
+            copy.wait()
+        if event < 3:
+            self.held[...] = self.held[...] + self.landing[event]
+            for copy in self._copies(event + 1):
+                copy.start()
+        else:
+            self.landing[3 + self.place.at["z"]] = self.held[...]
+            lower, upper = self.landing[3] + self.landing[4], self.landing[5] + self.landing[6]
+            self.held[...] = lower + upper
+
+
+def normed(hidden, gain, shift):
+    center = hidden - jnp.mean(hidden, axis=-1, keepdims=True)
+    scale = lax.rsqrt(jnp.mean(center * center, axis=-1, keepdims=True) + 1e-05)
+    unit = center * scale
+    return unit * gain + shift, unit, scale
+
+
+def normed_back(grad, unit, scale, gain):
+    d_unit = grad * gain
+    mean = jnp.mean(d_unit, axis=-1, keepdims=True)
+    slope = jnp.mean(d_unit * unit, axis=-1, keepdims=True)
+    d_hidden = scale * (d_unit - mean - unit * slope)
+    return d_hidden, jnp.sum(grad * unit, axis=0, keepdims=True), jnp.sum(grad, axis=0, keepdims=True)
+
+
+WEIGHTS = dict(
+    self_query=(MODEL, MODEL),
+    self_key=(MODEL, MODEL),
+    self_value=(MODEL, MODEL),
+    self_out=(MODEL, MODEL),
+    cross_query=(MODEL, MODEL),
+    cross_key=(MODEL, MODEL),
+    cross_value=(MODEL, MODEL),
+    cross_out=(MODEL, MODEL),
+    expand_weight=(MODEL, HIDDEN),
+    reduce_weight=(HIDDEN, MODEL),
+)
+LEFT = dict(states=512, attended=512, first=512, crossed=512, second=512, hidden=2048)
+RIGHT = dict(d_branch=512, d_gate=2048, d_cross=512, d_cross_q=512, d_self=512, d_q=512, d_k=512, d_v=512)
+
+
+def scratch_of():
+    f32 = jnp.float32
+    shapes = dict(
+        q_out=((CHIPS, 64, 128), LOW),
+        q_in=((CHIPS, 64, 128), LOW),
+        q_pad=((CHIPS, 128, 128), LOW),
+        kv_out=((CHIPS, 144, 128), LOW),
+        kv_in=((2 * CHIPS, 144, 128), LOW),
+        mem_out=((16, 256), LOW),
+        mem_in=((2, CHIPS, 16, 256), LOW),
+        mem_f32=((TOKENS, MODEL), f32),
+        mem_rows=((2, TOKENS, MODEL), LOW),
+        mem_k=((TOKENS, MODEL), LOW),
+        mem_v=((TOKENS, MODEL), LOW),
+        ids=((16, 128), f32),
+        probs=((CHIPS, 128, 2048), LOW),
+        accum=((CHIPS, 128, 128), f32),
+        a_out=((CHIPS, 64, 128), LOW),
+        a_in=((CHIPS, 64, 128), LOW),
+        da_out=((CHIPS, 64, 128), LOW),
+        da_in=((CHIPS, 64, 128), LOW),
+        dq_out=((CHIPS, 64, 128), LOW),
+        dq_in=((CHIPS, 64, 128), LOW),
+        dkv_out=((CHIPS, 128, 128), LOW),
+        dkv_in=((CHIPS, 128, 128), LOW),
+        dkv=((2 * CHIPS, 128, 128), f32),
+        dkv_pair=((CHIPS, 128, 128), f32),
+        gate=((TOKENS, HIDDEN), f32),
+        cross_p=((8 * TOKENS, 128), f32),
+        cross_q=((TOKENS, MODEL), LOW),
+        crossed_d=((TOKENS, MODEL), LOW),
+        d_mem=((2, TOKENS, MODEL), f32),
+        d_mem_out=((2, TOKENS, 256), LOW),
+        d_mem_pair=((2, TOKENS, 256), LOW),
+        part=((SUMMED_ROWS, 256), LOW),
+        landing=((SUMMED_ROWS * 15 // 16, 256), LOW),
+        done=((2, DONE_ROWS, 256), LOW),
+        rows_held=((SLOTS, MODEL), f32),
+        rows_in=((7, SLOTS, MODEL), f32),
+        d_start=((TOKENS, MODEL), f32),
+    )
+    for name, width in LEFT.items():
+        shapes["left_" + name] = ((2 * TOKENS, width), LOW)
+    for name, width in RIGHT.items():
+        shapes["full_" + name] = ((TOKENS, width), LOW)
+        shapes["right_" + name] = ((2 * TOKENS, width // 2), LOW)
+    for name, shape in WEIGHTS.items():
+        shapes["w_" + name] = (shape, LOW)
+    return shapes
+
+
+VECTORS = tuple(name for name in inspect.signature(body).parameters if name[:4] in ("gain", "shif"))
+GIVEN = ("states", "memory", "target_segments", "memory_segments", "output_cotangent") + VECTORS
+MADE = ("layer_output", "states_grad", "memory_grad", "rows", "sums")
+
+
+def layer_kernel(*refs):
+    names = GIVEN + tuple(WEIGHTS) + MADE + tuple(scratch_of()) + ("send", "recv", "fetch")
+    assert len(names) == len(refs)
+    r = types.SimpleNamespace(**dict(zip(names, refs)))
+    place = Place()
+    links = Links(place, r.send, r.recv)
+    row, seq, core, chip = place.row, place.seq, place.core, place.chip
+    scale = HEAD_DIM**-0.5
+    f32 = jnp.float32
+
+    fetches = {}
+    for number, name in enumerate(WEIGHTS):
+        fetches[name] = pltpu.make_async_copy(getattr(r, name), getattr(r, "w_" + name), r.fetch.at[number])
+        fetches[name].start()
+
+    def weight(name):
+        if fetches.get(name) is not None:
+            fetches[name].wait()
+            fetches[name] = None
+        return getattr(r, "w_" + name)
+
+    barrier = pltpu.get_barrier_semaphore()
+    friends = [place.sibling(), place.moved("x", 1)[1]]
+    friends += [place.on_chip(lax.rem(chip + hop, CHIPS)) for hop in range(1, CHIPS)]
+    for friend in friends:
+        pl.semaphore_signal(barrier, inc=1, device_id=friend, device_id_type=MESH)
+
+    own_rows = pl.ds(pl.multiple_of(core * TOKENS, TOKENS), TOKENS)
+    lefts, rights = {}, {}
+
+    def give_left(name):
+        ref = getattr(r, "left_" + name).at[own_rows]
+        lefts[name] = Pair(links, ref, ref)
+        lefts[name].start()
+
+    def left(name):
+        if lefts[name] is not None:
+            lefts[name].wait()
+            lefts[name] = None
+        return getattr(r, "left_" + name)
+
+    def give_right(name):
+        full, both = getattr(r, "full_" + name), getattr(r, "right_" + name)
+        half = RIGHT[name] // 2
+        other = full.at[:, pl.ds(pl.multiple_of((1 - core) * half, half), half)]
+        both[own_rows, :] = full[:, pl.ds(pl.multiple_of(core * half, half), half)]
+        rights[name] = Pair(links, other, both.at[own_rows])
+        rights[name].start()
+
+    def right(name):
+        if rights[name] is not None:
+            rights[name].wait()
+            rights[name] = None
+        return getattr(r, "right_" + name)
+
+    tokens = r.states[...]
+    r.left_states[own_rows, :] = tokens
+    queries = dot(tokens, weight("self_query")[...]) * scale
+    keys = dot(tokens, weight("self_key")[...])
+    values = dot(tokens, weight("self_value")[...])
+    r.ids[...] = jnp.zeros((16, 128), f32)
+    r.ids[0:1, :] = r.target_segments[...].astype(f32)
+    r.ids[1:2, 0:8] = r.memory_segments[...].astype(f32)
+    ids = r.ids[...].astype(LOW)
+    left128 = left_lanes(128)
+    for pair in range(4):
+        lanes = slice(128 * pair, 128 * pair + 128)
+        even, odd = fold_pair(queries[:, lanes])
+        r.q_out[2 * pair] = even.astype(LOW)
+        r.q_out[2 * pair + 1] = odd.astype(LOW)
+        key_pair, value_pair = keys[:, lanes], values[:, lanes]
+        r.kv_out[2 * pair, 0:128] = jnp.where(left128, key_pair, turned(value_pair)).astype(LOW)
+        r.kv_out[2 * pair + 1, 0:128] = jnp.where(left128, turned(key_pair), value_pair).astype(LOW)
+        r.kv_out[2 * pair, 128:144] = ids
+        r.kv_out[2 * pair + 1, 128:144] = ids
+    memory = r.memory[...].astype(f32)
+    r.mem_out[...] = jnp.concatenate([memory[:, :256], memory[:, 256:]], axis=0).astype(LOW)
+
+    pl.semaphore_wait(barrier, len(friends))
+    kv_base = links.take(CHIPS)
+    kv_send = links.take(CHIPS)
+
+    def kv_copy(hop):
+        there = lax.rem(chip + hop, CHIPS)
+        return links.copy(r.kv_out.at[there], r.kv_in.at[seq], place.on_chip(there), kv_send + hop, kv_base + chip)
+
+    def kv_own():
+        return links.local(r.kv_out.at[chip], r.kv_in.at[seq], kv_base + chip)
+
+    kv_own().start()
+    for hop in range(1, CHIPS):
+        kv_copy(hop).start()
+    q_spread = Spread(links, r.q_out, r.q_in)
+    q_spread.start_all()
+    mem_base = links.take(CHIPS)
+    mem_send = links.take(CHIPS)
+
+    def mem_copy(hop):
+        there = lax.rem(chip + hop, CHIPS)
+        return links.copy(r.mem_out, r.mem_in.at[core, chip], place.on_chip(there), mem_send + hop, mem_base + chip)
+
+    def mem_own():
+        return links.local(r.mem_out, r.mem_in.at[core, chip], mem_base + chip)
+
+    mem_own().start()
+    for hop in range(1, CHIPS):
+        mem_copy(hop).start()
+    give_left("states")
+
+    kv_on = [Pair(links, r.kv_in.at[2 * source + core], r.kv_in.at[2 * source + core]) for source in range(CHIPS)]
+
+    def kv_pass(source):
+        slot = r.kv_in.at[2 * source + core]
+        links.local(slot, slot, kv_base + source).wait()
+        kv_on[source].start()
+
+    def count(slot, line, number):
+        found = r.kv_in[slot, 128:144].astype(f32)[line : line + 1]
+        return jnp.sum(jnp.where(found == number, 1.0, 0.0), axis=1, keepdims=True)
+
+    def first_seen(position, first_one, first_two):
+        if first_two is None:
+            return jnp.where(position < first_one, 0.0, first_one)
+        return jnp.where(position < first_one, 0.0, jnp.where(position < first_two, first_one, first_two))
+
+    kv_pass(0)
+    a_spread = Spread(links, r.a_out, r.a_in)
+    length = 2 * CHIPS * TOKENS
+    for source in range(CHIPS):
+        if source + 1 < CHIPS:
+            kv_pass(source + 1)
+        q_spread.wait_from(source)
+        kv_on[source].wait()
+        width = 256 * (source + 1)
+        folded = r.q_in[source].astype(f32)
+        left64 = left_lanes(64)
+        padded = jnp.concatenate([jnp.where(left64, folded, 0.0), jnp.where(left64, turned(folded), 0.0)], axis=0)
+        padded = padded.astype(LOW)
+        r.q_pad[source] = padded
+        both = r.kv_in[0 : 2 * source + 2, 0:128].reshape(width, 128)
+        scores = dot_rows(padded, both)
+        place_q = (core * TOKENS + 2 * source * TOKENS + lax.broadcasted_iota(jnp.int32, (128, 1), 0)).astype(f32)
+        place_k = lax.broadcasted_iota(jnp.int32, (128, width), 1).astype(f32)
+        first_one = count(0, 0, 0)
+        first_two = length - count(2 * CHIPS - 1, 0, 2) if source == CHIPS - 1 else None
+        allowed = (place_k >= first_seen(place_q, first_one, first_two)) & (place_k <= place_q)
+        scores = jnp.where(allowed, scores, -1e30)
+        weights = jnp.exp(scores - jnp.max(scores, axis=1, keepdims=True))
+        probs = (weights / jnp.sum(weights, axis=1, keepdims=True)).astype(LOW)
+        r.probs[source, :, 0:width] = probs
+        attended = dot(probs, both)
+        r.accum[source] = attended
+        r.a_out[source] = jnp.where(left64, turned(attended[:64]), attended[64:]).astype(LOW)
+        a_spread.start(source)
+
+    for source in range(CHIPS):
+        slot = r.mem_in.at[core, source]
+        links.local(slot, slot, mem_base + source).wait()
+    mem_pair = Pair(links, r.mem_in.at[core], r.mem_in.at[core])
+    mem_pair.start()
+    mem_pair.wait()
+    for source in range(CHIPS):
+        for side in range(2):
+            found = r.mem_in[side, source].astype(f32)
+            at = (2 * source + side) * 8
+            r.mem_f32[at : at + 8, 0:256] = found[0:8]
+            r.mem_f32[at : at + 8, 256:512] = found[8:16]
+    mem_all = r.mem_f32[...].astype(LOW)
+    r.mem_rows[row] = mem_all
+    mem_x_sem = links.take(1)
+    mem_x = links.copy(r.mem_rows.at[row], r.mem_rows.at[row], place.moved("x", 1)[1], mem_x_sem, mem_x_sem)
+    mem_x.start()
+    r.mem_k[...] = dot(mem_all, weight("cross_key")[...]).astype(LOW)
+    r.mem_v[...] = dot(mem_all, weight("cross_value")[...]).astype(LOW)
+
+    for source in range(CHIPS):
+        a_spread.wait_from(source)
+    for pair in range(4):
+        block = unfold_pair(r.a_in[2 * pair].astype(f32), r.a_in[2 * pair + 1].astype(f32))
+        r.left_attended[own_rows, 128 * pair : 128 * pair + 128] = block.astype(LOW)
+    give_left("attended")
+    gains = types.SimpleNamespace(**{name: getattr(r, name)[...].reshape(1, MODEL) for name in VECTORS})
+    attended = r.left_attended[own_rows, :]
+    first, unit_one, scale_one = normed(
+        tokens.astype(f32) + dot(attended, weight("self_out")[...]), gains.gain_one, gains.shift_one
+    )
+    first_low = first.astype(LOW)
+    r.left_first[own_rows, :] = first_low
+    give_left("first")
+    r.cross_q[...] = (dot(first_low, weight("cross_query")[...]) * scale).astype(LOW)
+
+    place_q = (seq * TOKENS + lax.broadcasted_iota(jnp.int32, (128, 1), 0)).astype(f32)
+    first_one, first_two = count(0, 0, 0), length - count(2 * CHIPS - 1, 0, 2)
+    mem_one, mem_two = count(0, 1, 0), TOKENS - count(2 * CHIPS - 1, 1, 2)
+    mem_one = mem_one - (TOKENS - 8)
+    id_q = jnp.where(place_q < first_one, 0.0, jnp.where(place_q < first_two, 1.0, 2.0))
+    place_m = lax.broadcasted_iota(jnp.int32, (1, 128), 1).astype(f32)
+    id_m = jnp.where(place_m < mem_one, 0.0, jnp.where(place_m < mem_two, 1.0, 2.0))
+    seen = id_q == id_m
+    seen = jnp.concatenate([seen.astype(f32), seen.astype(f32)], axis=0) > 0.5
+
+    def stacked(block):
+        zero = jnp.zeros_like(block)
+        return jnp.concatenate([jnp.where(left128, block, zero), jnp.where(left128, zero, block)], axis=0)
+
+    for pair in range(4):
+        lanes = slice(128 * pair, 128 * pair + 128)
+        scores = dot_rows(stacked(r.cross_q[:, lanes]), r.mem_k[:, lanes])
+        scores = jnp.where(seen, scores, -1e30)
+        weights = jnp.exp(scores - jnp.max(scores, axis=1, keepdims=True))
+        probs = weights / jnp.sum(weights, axis=1, keepdims=True)
+        r.cross_p[256 * pair : 256 * pair + 256] = probs
+        mixed = dot(probs.astype(LOW), r.mem_v[:, lanes])
+        r.left_crossed[own_rows, lanes] = jnp.where(left128, mixed[:128], mixed[128:]).astype(LOW)
+    give_left("crossed")
+    crossed = r.left_crossed[own_rows, :]
+    second, unit_two, scale_two = normed(first + dot(crossed, weight("cross_out")[...]), gains.gain_two, gains.shift_two)
+    second_low = second.astype(LOW)
+    r.left_second[own_rows, :] = second_low
+    give_left("second")
+    third = second
+    for number in range(4):
+        wide = slice(512 * number, 512 * number + 512)
+        gate = dot(second_low, weight("expand_weight")[:, wide])
+        sigma = 1.0 / (1.0 + jnp.exp(-gate))
+        hidden = (gate * sigma).astype(LOW)
+        r.gate[:, wide] = sigma * (1.0 + gate * (1.0 - sigma))
+        r.left_hidden[own_rows, wide] = hidden
+        third = third + dot(hidden, weight("reduce_weight")[wide, :])
+    give_left("hidden")
+    result, unit_three, scale_three = normed(third, gains.gain_three, gains.shift_three)
+    r.layer_output[...] = result.astype(LOW)
+
+    part = r.part
+    pieces, landing_at, start = [], 0, 0
+    for size in PIECES:
+        pieces.append(Summed(links, part, r.landing, r.done, start, size, landing_at))
+        landing_at, start = pieces[-1].landing_end, start + size
+    begun = []
+
+    def begin(number):
+        pieces[number].begin()
+        begun.append(number)
+
+    d_third, d_gain_three, d_shift_three = normed_back(
+        r.output_cotangent[...].astype(f32), unit_three, scale_three, gains.gain_three
+    )
+    d_branch = d_third.astype(LOW)
+    r.full_d_branch[...] = d_branch
+    give_right("d_branch")
+    d_second = d_third
+    for number in range(4):
+        wide = slice(512 * number, 512 * number + 512)
+        d_gate = (dot_rows(d_branch, weight("reduce_weight")[wide, :]) * r.gate[:, wide]).astype(LOW)
+        r.full_d_gate[:, wide] = d_gate
+        d_second = d_second + dot_rows(d_gate, weight("expand_weight")[:, wide])
+    give_right("d_gate")
+
+    def outer(at, left_name, columns, right_name, right_columns):
+        made = dot_tokens(left(left_name)[:, columns], right(right_name)[:, right_columns])
+        part[at : at + 512] = made.astype(LOW)
+
+    every, short = slice(0, 512), slice(0, 256)
+    for number in range(4):
+        outer(AT.reduce + 512 * number, "hidden", slice(512 * number, 512 * number + 512), "d_branch", short)
+        if number % 2 == 1:
+            begin(number // 2)
+    for number in range(4):
+        outer(AT.expand + 512 * number, "second", every, "d_gate", slice(256 * number, 256 * number + 256))
+        if number % 2 == 1:
+            begin(2 + number // 2)
+    d_mid, d_gain_two, d_shift_two = normed_back(d_second, unit_two, scale_two, gains.gain_two)
+    d_cross = d_mid.astype(LOW)
+    r.full_d_cross[...] = d_cross
+    give_right("d_cross")
+    r.crossed_d[...] = dot_rows(d_cross, weight("cross_out")[...]).astype(LOW)
+    for pair in range(4):
+        lanes = slice(128 * pair, 128 * pair + 128)
+        probs = r.cross_p[256 * pair : 256 * pair + 256]
+        d_out = stacked(r.crossed_d[:, lanes])
+        d_probs = dot_rows(d_out, r.mem_v[:, lanes])
+        delta = jnp.sum(probs * d_probs, axis=1, keepdims=True)
+        d_scores = (probs * (d_probs - delta)).astype(LOW)
+        mixed = dot(d_scores, r.mem_k[:, lanes]) * scale
+        r.full_d_cross_q[:, lanes] = jnp.where(left128, mixed[:128], mixed[128:]).astype(LOW)
+        r.d_mem[0, :, lanes] = dot_tokens(d_scores, stacked(r.cross_q[:, lanes]))
+        r.d_mem[1, :, lanes] = dot_tokens(probs.astype(LOW), d_out)
+    give_right("d_cross_q")
+    mine = pl.ds(pl.multiple_of(core * 256, 256), 256)
+    others = pl.ds(pl.multiple_of((1 - core) * 256, 256), 256)
+    r.d_mem_out[...] = r.d_mem[:, :, others].astype(LOW)
+    mem_grads = Pair(links, r.d_mem_out, r.d_mem_pair)
+    mem_grads.start()
+    d_first = d_mid + dot_rows(r.full_d_cross_q[...], weight("cross_query")[...])
+    d_start, d_gain_one, d_shift_one = normed_back(d_first, unit_one, scale_one, gains.gain_one)
+    r.d_start[...] = d_start
+    d_self = d_start.astype(LOW)
+    r.full_d_self[...] = d_self
+    give_right("d_self")
+    d_attended = dot_rows(d_self, weight("self_out")[...])
+    for pair in range(4):
+        even, odd = fold_pair(d_attended[:, 128 * pair : 128 * pair + 128])
+        r.da_out[2 * pair] = even.astype(LOW)
+        r.da_out[2 * pair + 1] = odd.astype(LOW)
+    da_spread = Spread(links, r.da_out, r.da_in)
+    da_spread.start_all()
+    made = [d_gain_one, d_shift_one, d_gain_two, d_shift_two, d_gain_three, d_shift_three]
+    r.rows_held[...] = jnp.concatenate(made + [jnp.zeros((2, MODEL), f32)], axis=0)
+    norm_rows = Rows(links, r.rows_held, r.rows_in)
+    norm_rows.begin()
+
+    outer(AT.cross_out, "crossed", every, "d_cross", short)
+    mem_grads.wait()
+    mem_at = AT.memory
+    for side in range(2):
+        total = r.d_mem[side, :, mine] + r.d_mem_pair[side].astype(f32)
+        part[rows_at(mem_at + row * 256 + side * 128, 128)] = total.astype(LOW)
+        part[rows_at(mem_at + (1 - row) * 256 + side * 128, 128)] = jnp.zeros((128, 256), LOW)
+    begin(4)
+    outer(AT.cross_query, "first", every, "d_cross_q", short)
+    outer(AT.self_out, "attended", every, "d_self", short)
+    begin(5)
+
+    waiting = {number: 0 for number in range(len(pieces))}
+    row_events = [0]
+
+    def advance(count):
+        for _ in range(count):
+            ready = [number for number in begun if waiting[number] < 7]
+            if not ready:
+                return
+            number = min(ready, key=lambda item: (item + 1.5 * waiting[item], item))
+            pieces[number].advance(waiting[number])
+            waiting[number] += 1
+
+    def advance_rows():
+        norm_rows.advance(row_events[0])
+        row_events[0] += 1
+
+    advance(2)
+    dq_spread = Spread(links, r.dq_out, r.dq_in)
+    dkv_spread = Spread(links, r.dkv_out, r.dkv_in)
+    dkv_pairs = {}
+
+    def dkv_finish(source):
+        dkv_pairs[source].wait()
+        r.dkv_out[source] = (r.dkv[2 * source + core] + r.dkv_pair[source]).astype(LOW)
+        dkv_spread.start(source)
+
+    for source in reversed(range(CHIPS)):
+        da_spread.wait_from(source)
+        width = 256 * (source + 1)
+        folded = r.da_in[source].astype(f32)
+        left64 = left_lanes(64)
+        d_out = jnp.concatenate([jnp.where(left64, 0.0, turned(folded)), jnp.where(left64, 0.0, folded)], axis=0)
+        delta = jnp.sum(d_out * r.accum[source], axis=1, keepdims=True)
+        d_out = d_out.astype(LOW)
+        both = r.kv_in[0 : 2 * source + 2, 0:128].reshape(width, 128)
+        d_probs = dot_rows(d_out, both)
+        probs = r.probs[source, :, 0:width]
+        d_scores = (probs.astype(f32) * (d_probs - delta)).astype(LOW)
+        d_query = dot(d_scores, both) * scale
+        r.dq_out[source] = jnp.where(left64, d_query[:64], turned(d_query[64:])).astype(LOW)
+        dq_spread.start(source)
+        d_both = dot_tokens(
+            jnp.concatenate([d_scores, probs], axis=0), jnp.concatenate([r.q_pad[source], d_out], axis=0)
+        ).reshape(2 * source + 2, 128, 128)
+        if source == CHIPS - 1:
+            r.dkv[...] = d_both
+        else:
+            r.dkv[0 : 2 * source + 2] = r.dkv[0 : 2 * source + 2] + d_both
+        dkv_pairs[source] = Pair(links, r.dkv.at[2 * source + 1 - core], r.dkv_pair.at[source])
+        dkv_pairs[source].start()
+        if source + 1 < CHIPS:
+            dkv_finish(source + 1)
+        advance(2)
+        if source % 2 == 0:
+            advance_rows()
+    dkv_finish(0)
+
+    for source in range(CHIPS):
+        dq_spread.wait_from(source)
+        dkv_spread.wait_from(source)
+    for pair in range(4):
+        lanes = slice(128 * pair, 128 * pair + 128)
+        block = unfold_pair(r.dq_in[2 * pair].astype(f32), r.dq_in[2 * pair + 1].astype(f32))
+        r.full_d_q[:, lanes] = block.astype(LOW)
+        even, odd = r.dkv_in[2 * pair].astype(f32), r.dkv_in[2 * pair + 1].astype(f32)
+        r.full_d_k[:, lanes] = jnp.where(left128, even, turned(odd)).astype(LOW)
+        r.full_d_v[:, lanes] = jnp.where(left128, turned(even), odd).astype(LOW)
+    for name in ("d_q", "d_k", "d_v"):
+        give_right(name)
+    for name, kind in (("d_q", "self_query"), ("d_k", "self_key"), ("d_v", "self_value")):
+        outer(getattr(AT, kind), "states", every, name, short)
+    begin(6)
+    grad = r.d_start[...]
+    for name, kind in (("d_q", "self_query"), ("d_k", "self_key"), ("d_v", "self_value")):
+        grad = grad + dot_rows(getattr(r, "full_" + name)[...], weight(kind)[...])
+    r.states_grad[...] = grad
+
+    done, sums = r.done, r.sums
+    mem_x.wait()
+    out_base = links.take(len(pieces) + 1)
+    outs = []
+
+    def put(start, size):
+        rows = pl.ds(start, size)
+        copy = links.local(done.at[:, rows], sums.at[:, rows], out_base + len(outs))
+        copy.start()
+        outs.append(copy)
+
+    written = set()
+
+    def flush():
+        for number, piece in enumerate(pieces):
+            if waiting[number] == 7 and number not in written:
+                put(piece.start, piece.size)
+                written.add(number)
+
+    extra = []
+
+    def memory_sums():
+        mems = r.mem_rows[...].reshape(2 * TOKENS, MODEL)
+        for side, kind in ((0, "cross_key"), (1, "cross_value")):
+            grads = [done[core, mem_at + 256 * number + 128 * side : mem_at + 256 * number + 128 * side + 128] for number in range(2)]
+            made = dot_tokens(mems, jnp.concatenate(grads, axis=0))
+            done[core, getattr(AT, kind) : getattr(AT, kind) + 512] = made.astype(LOW)
+        mine = done.at[core, pl.ds(SUMMED_ROWS, DONE_ROWS - SUMMED_ROWS)]
+        extra.append(Pair(links, mine, mine))
+        extra[0].start()
+
+    def memory_out():
+        grads = []
+        for side in range(2):
+            rows = rows_at(mem_at + row * 256 + side * 128 + chip * 16, 16)
+            grads.append(jnp.concatenate([done[0, rows], done[1, rows]], axis=1))
+        both = dot_rows(grads[0], weight("cross_key")[...]) + dot_rows(grads[1], weight("cross_value")[...])
+        r.memory_grad[...] = jnp.where(core == 0, both[0:8], both[8:16])
+        extra[0].wait()
+        put(SUMMED_ROWS, DONE_ROWS - SUMMED_ROWS)
+
+    while any(count < 7 for count in waiting.values()):
+        before = waiting[4]
+        advance(1)
+        if before < 6 and waiting[4] == 6:
+            memory_sums()
+        if before < 7 and waiting[4] == 7:
+            memory_out()
+        flush()
+    r.rows[...] = r.rows_held[...]
+    for hop in range(1, CHIPS):
+        kv_copy(hop).wait_send()
+        mem_copy(hop).wait_send()
+    q_spread.end_all()
+    da_spread.end_all()
+    for source in range(CHIPS):
+        a_spread.end(source)
+        dq_spread.end(source)
+        dkv_spread.end(source)
+    for copy in outs:
+        copy.wait()
+
+
+def finish_kernel(rows, sums, *refs):
+    names = tuple(WEIGHTS) + VECTORS
+    out = dict(zip(names, refs))
+    low, wide, fetch, store = refs[len(names) :]
+    blocks = []
+    for core in range(2):
+        for number in range(4):
+            blocks.append((core, AT.reduce + 512 * number, "reduce_weight", 512 * number, 256 * core))
+            blocks.append((core, AT.expand + 512 * number, "expand_weight", 0, 1024 * core + 256 * number))
+        for name in WEIGHTS:
+            if hasattr(AT, name):
+                blocks.append((core, getattr(AT, name), name, 0, 256 * core))
+    reads, writes = [], []
+    for number, (core, at, name, down, along) in enumerate(blocks):
+        reads.append(pltpu.make_async_copy(sums.at[core, pl.ds(at, 512)], low.at[number], fetch.at[number]))
+        there = out[name].at[pl.ds(down, 512), pl.ds(along, 256)]
+        writes.append(pltpu.make_async_copy(wide.at[number], there, store.at[number]))
+    for read in reads:
+        read.start()
+    for number, name in enumerate(VECTORS):
+        out[name][...] = rows[number, :]
+    for number, (read, write) in enumerate(zip(reads, writes)):
+        read.wait()
+        wide[number] = low[number].astype(jnp.float32)
+        write.start()
+    for write in writes:
+        write.wait()
+
+
+def fast_body(*given):
+    names = tuple(inspect.signature(body).parameters)
+    arrays = dict(zip(names, given))
+    for name in ("states", "memory", "output_cotangent"):
+        arrays[name] = arrays[name][0]
+    vmem = pl.BlockSpec(memory_space=pltpu.VMEM)
+    hbm = pl.BlockSpec(memory_space=pl.ANY)
+    f32 = jnp.float32
+    semaphores = pltpu.SemaphoreType.DMA((SEMAPHORES,))
+    layer_output, states_grad, memory_grad, rows, sums = pl.pallas_call(
+        layer_kernel,
+        out_shape=(
+            jax.ShapeDtypeStruct((TOKENS, MODEL), LOW),
+            jax.ShapeDtypeStruct((TOKENS, MODEL), f32),
+            jax.ShapeDtypeStruct((8, MODEL), f32),
+            jax.ShapeDtypeStruct((SLOTS, MODEL), f32),
+            jax.ShapeDtypeStruct((2, DONE_ROWS, 256), LOW),
+        ),
+        in_specs=[vmem] * len(GIVEN) + [hbm] * len(WEIGHTS),
+        out_specs=(vmem, vmem, vmem, vmem, hbm),
+        scratch_shapes=[pltpu.VMEM(shape, kind) for shape, kind in scratch_of().values()]
+        + [semaphores, semaphores, pltpu.SemaphoreType.DMA((len(WEIGHTS),))],
+        compiler_params=pltpu.CompilerParams(collective_id=0, has_side_effects=True, vmem_limit_bytes=60 << 20),
+    )(*[arrays[name] for name in GIVEN], *[arrays[name] for name in WEIGHTS])
+    blocks = 32
+    made = pl.pallas_call(
+        finish_kernel,
+        out_shape=tuple(jax.ShapeDtypeStruct(shape, f32) for shape in WEIGHTS.values())
+        + tuple(jax.ShapeDtypeStruct((MODEL,), f32) for _ in VECTORS),
+        in_specs=[vmem, hbm],
+        out_specs=tuple([hbm] * len(WEIGHTS) + [vmem] * len(VECTORS)),
+        scratch_shapes=[
+            pltpu.VMEM((blocks, 512, 256), LOW),
+            pltpu.VMEM((blocks, 512, 256), f32),
+            pltpu.SemaphoreType.DMA((blocks,)),
+            pltpu.SemaphoreType.DMA((blocks,)),
+        ],
+        compiler_params=pltpu.CompilerParams(vmem_limit_bytes=48 << 20),
+    )(rows, sums)
+    grads = dict(zip(tuple(WEIGHTS) + VECTORS, made))
+    return (layer_output[None], states_grad[None], memory_grad[None]) + tuple(grads[name] for name in names[4:-1])
+
+
 def solution(mesh):
+    def either(*given):
+        shapes = [given[0].shape, given[1].shape, given[16].shape]
+        fits = shapes == [(1, TOKENS, MODEL), (1, 8, MODEL), (MODEL, HIDDEN)]
+        fits = fits and dict(mesh.shape) == {ROWS: EXTENT["x"], SEQ: 2 * CHIPS}
+        return (fast_body if fits else body)(*given)
+
     return jax.shard_map(
-        body,
+        either,
         mesh=mesh,
         in_specs=(
-            P("rows", "seq", None),
-            P("rows", "seq", None),
-            P("rows", "seq"),
-            P("rows", "seq"),
-            P(),
-            P(),
-            P(),
-            P(),
-            P(),
-            P(),
-            P(),
-            P(),
-            P(),
-            P(),
-            P(),
-            P(),
-            P(),
-            P(),
-            P(),
-            P(),
-            P("rows", "seq", None),
+            P(ROWS, SEQ, None),
+            P(ROWS, SEQ, None),
+            P(ROWS, SEQ),
+            P(ROWS, SEQ),
+            P(),
+            P(),
+            P(),
+            P(),
+            P(),
+            P(),
+            P(),
+            P(),
+            P(),
+            P(),
+            P(),
+            P(),
+            P(),
+            P(),
+            P(),
+            P(),
+            P(ROWS, SEQ, None),
         ),
         out_specs=(
-            P("rows", "seq", None),
-            P("rows", "seq", None),
-            P("rows", "seq", None),
+            P(ROWS, SEQ, None),
+            P(ROWS, SEQ, None),
+            P(ROWS, SEQ, None),
             P(),
             P(),
             P(),

time: 864 us -> 152 us (0.18)
  waiting for transfers between devices: 333 us -> 0 us
  blocking collectives: 193 us -> 0 us
  Pallas kernels: 0 us -> 148 us
  matrix products: 145 us -> 0 us
  local copies, waits for them, and re-layouts: 102 us -> 2.69 us
  loops' own time: 42.1 us -> 0 us
  other arithmetic: 24.6 us -> 0 us
  between operations: 19 us -> 0.7 us
    psum x1 -> x0, waiting for transfers between devices: 249 us -> none  [body(): lax.psum((self_query_grad, self_key_grad, self_value_grad, self_out_grad,...]
    pallas_call x0 -> x2, Pallas kernels: none -> 148 us  [the longest x1 139 us: fast_body(): pl.pallas_call(layer_kernel, out_shape=(jax.ShapeDtypeStruct((TOKENS, MOD...]
    dot_general x87 -> x0, matrix products: 142 us -> none  [the longest x16 33.6 us: key_part(): jnp.einsum('qhk,qhd->khd', grads_s, piece_query_heads, preferred_element_...]
    all_gather x5 -> x0, blocking collectives: 102 us -> none  [the longest x1 23.8 us: body(): piece_seg = lax.all_gather(query_seg, 'seq', axis=0, tiled=True)]
    psum x1 -> x0, blocking collectives: 82.9 us -> none  [body(): lax.psum((self_query_grad, self_key_grad, self_value_grad, self_out_grad,...]
    unnamed x9 -> x0, waiting for transfers between devices: 43.8 us -> none
    another operation x18 -> x0, loops' own time: 42.1 us -> none  [the longest x1 40.8 us: both_sides(): return lax.fori_loop(0, shards, one_shard, grads)]
    all_gather x4 -> x0, waiting for transfers between devices: 40.7 us -> none  [the longest x1 39.1 us: body(): lax.all_gather(d_attended, 'seq', axis=0, tiled=True)]
  transfers between devices with their start and end apart: 7 -> 0, of which waited for: 4 -> 0; matrix products, arithmetic and copies ran while one was open for 12% -> 0% of each run, Pallas kernels for 0% -> 0%
where the time goes in v2:
time: 152 us
  Pallas kernels  148 us (97%)
  local copies, waits for them, and re-layouts  2.69 us (2%)
    pallas_call x1, Pallas kernels, fast_body(): pl.pallas_call(layer_kernel, out_shape=(jax.ShapeDtypeStruct((TOKENS, MOD...  139 us
    pallas_call x1, Pallas kernels, fast_body(): pl.pallas_call(finish_kernel, out_shape=tuple((jax.ShapeDtypeStruct(shape...  9.29 us

profile of v2, /device:TPU:0, one launch (start us, length us, event | category | flops | bytes accessed | tf_op | source)
XLA Modules:
  0.0 151.7 jit_solution(14449131786338365407)
XLA Ops:
  0.7 139.0 %shard_map.348 = (bf16[128,512]{1,0:T(8,128)(2,1)}, f32[128,512]{1,0:T(8,128)}, f32[8,512]{1,0:T(8,128)}, f32[8,512]{1,0:T(8,128)}, bf16[2,8704,256]{2,1,0:T(8,128)(2,1)}) custom-call(bf16[128,512]{1,0:T(8,128)(2,1)} %bitcast.7, bf16[8,512]{1,0:T(8,128)(2,1)} %bitcast.11, s32[1,128]{1,0:T(1,128)} %refs_2_.1, s32[1,8]{1,0:T(1,128)} %refs_3_.1, ...), custom_call_target="tpu_custom_call" | custom-call | tf_op jit(solution)/shard_map/pallas_call | solution.py:1313
  139.7 0.0 copy-start
  139.7 0.7 copy-done
  140.4 0.0 copy-start.2
  140.4 0.0 copy-start.1
  140.4 0.0 copy-start.3
  140.4 9.3 %shard_map.349 = (f32[512,512]{1,0:T(8,128)}, f32[512,512]{1,0:T(8,128)}, f32[512,512]{1,0:T(8,128)}, f32[512,512]{1,0:T(8,128)}, f32[512,512]{1,0:T(8,128)}, /*...) custom-call(f32[8,512]{1,0:T(8,128)S(1)} %copy-done, ...), custom_call_target="tpu_custom_call" | custom-call | tf_op jit(solution)/shard_map/pallas_call | solution.py:1329
  149.7 0.0 copy-done.2
  149.7 0.7 copy.43
  150.4 0.0 copy-done.1
  150.4 0.7 copy.44
  151.1 0.0 copy-done.3
  151.1 0.6 copy.45
Async XLA Ops:
  139.7 0.7 copy-start
  140.4 9.3 %copy-start.2 = (bf16[128,512]{1,0:T(8,128)(2,1)S(1)}, bf16[128,512]{1,0:T(8,128)(2,1)}, u32[]{:S(2)}) copy-start(bf16[128,512]{1,0:T(8,128)(2,1)} %get-tuple-element.40) | copy-start | bytes 393220
  140.4 10.0 %copy-start.1 = (f32[128,512]{1,0:T(8,128)S(1)}, f32[128,512]{1,0:T(8,128)}, u32[]{:S(2)}) copy-start(f32[128,512]{1,0:T(8,128)} %get-tuple-element.41) | copy-start | bytes 786436
  140.4 10.7 %copy-start.3 = (f32[8,512]{1,0:T(8,128)S(1)}, f32[8,512]{1,0:T(8,128)}, u32[]{:S(2)}) copy-start(f32[8,512]{1,0:T(8,128)} %get-tuple-element.42) | copy-start | bytes 49156
